TPU v7x, 256 devices: a whole 4x4x8 slice. The times are simulated.
256 devices in a mesh: dp: 32 (over x, z), mp: 8 (over y, core).
Axes of the slice: x: 4, y: 4, z: 8, core: 2. Of those that a mesh axis runs over, the one named last changes fastest.
Arguments:
- tiles: bfloat16 [512, 8, 3200], P('dp', None, 'mp'), may hold values from -6 to 6
- tile_counts: int32 [64], replicated, may hold values from 5 to 8, as said below
- encoder_rank: int32 [512], replicated, may hold values from 0 to 31, as said below
- out_grad: bfloat16 [512, 8, 3200], P('dp', None, 'mp'), may hold values from -6 to 6
- norm_gain: float32 [3200], replicated, may hold values from 0.5 to 1.5
- layer_scale: float32 [3200], replicated, may hold values from 0.4 to 1.6
- up_weight: bfloat16 [3200, 6400], P(None, 'mp'), may hold values from -0.109375 to 0.109375
- down_weight: bfloat16 [3200, 6400], P(None, 'mp'), may hold values from -0.078125 to 0.078125
Outputs:
- embedded: bfloat16 [512, 8, 3200], P('dp', None, 'mp')
- tile_grads: bfloat16 [512, 8, 3200], P('dp', None, 'mp')
- weight_grads: bfloat16 [3200, 6400], P('dp', 'mp')
Inputs may be any that keep to these rules, and one draw needn't show every extreme that they name: Sample i's tiles occupy the first tile_counts[i] of its 8 slots; some sample has exactly 8 tiles. `encoder_rank`: among live slots, no data rank sends two tiles to the same encoder rank; every encoder rank receives at most 16 live tiles and some encoder rank receives exactly 16.
All inputs are finite; a program needn't handle non-finite values.
Results may differ from a plain program's by a relative error of at most 0.029.
Values may be sent and summed in bfloat16 or wider, within the bound.
A program may use at most 64 MiB of HBM per device.

v0:
```python
import jax
import jax.numpy as jnp
from jax import lax
from jax.sharding import PartitionSpec as P

norm_eps = 1e-06
half_root = 0.7071067811865476
pdf_scale = 0.3989422804014327


def gelu_slope(values):
    return (
        0.5 * (1.0 + jax.scipy.special.erf(values * half_root))
        + values * jnp.exp(-0.5 * values * values) * pdf_scale
    )


def column_product(left, right):
    return lax.dot_general(
        left, right, (((0,), (0,)), ((), ())), preferred_element_type=jnp.float32
    )


def local(
    tiles, tile_counts, encoder_rank, out_grad, norm_gain, layer_scale, up_weight, down_weight
):
    groups = lax.axis_size("dp")
    slot_count = tiles.shape[0]
    tile_rows = tiles.shape[1]
    local_width = tiles.shape[2]
    per_sample = tile_counts.shape[0] // groups
    max_tiles = slot_count // per_sample
    my_rank = lax.axis_index("dp")
    slot_index = jnp.arange(slot_count, dtype=jnp.int32)
    peer_ids = jnp.arange(groups, dtype=jnp.int32)
    counts = tile_counts.reshape(groups, per_sample)
    sample_hot = (
        (slot_index // max_tiles)[:, None] == jnp.arange(per_sample, dtype=jnp.int32)[None, :]
    ).astype(jnp.int32)
    per_slot = jnp.sum(counts[:, None, :] * sample_hot[None, :, :], axis=2)
    is_live = (slot_index % max_tiles)[None, :] < per_slot
    dest_table = encoder_rank.reshape(groups, slot_count)
    my_live = lax.dynamic_index_in_dim(is_live, my_rank, 0, keepdims=False)
    my_table = lax.dynamic_index_in_dim(dest_table, my_rank, 0, keepdims=False)
    picker = ((my_table[None, :] == peer_ids[:, None]) & my_live[None, :]).astype(jnp.bfloat16)
    outgoing = jnp.einsum("es,srd->erd", picker, tiles, preferred_element_type=jnp.float32).astype(
        jnp.bfloat16
    )
    incoming = lax.all_to_all(outgoing, "dp", split_axis=0, concat_axis=0, tiled=True)
    arrives = jnp.any((dest_table == my_rank) & is_live, axis=1).astype(jnp.int32)
    arrival_rank = jnp.cumsum(arrives) - arrives
    packer = ((arrival_rank[None, :] == slot_index[:, None]) & (arrives[None, :] > 0)).astype(
        jnp.bfloat16
    )
    local_x = jnp.einsum(
        "ks,srd->krd", packer, incoming, preferred_element_type=jnp.float32
    ).astype(jnp.bfloat16)
    filled = slot_index < jnp.sum(arrives)
    total_rows = slot_count * tile_rows
    row_mask = jnp.repeat(filled, tile_rows).astype(jnp.float32)[:, None]
    local_grad = jnp.where(filled[:, None, None], out_grad, jnp.zeros_like(out_grad))
    full_x, full_grad = (
        lax.all_gather(local_x, "mp", axis=2, tiled=True),
        lax.all_gather(local_grad, "mp", axis=2, tiled=True),
    )
    x_float = full_x.reshape(total_rows, -1).astype(jnp.float32)
    radius = lax.rsqrt(jnp.mean(x_float * x_float, axis=1, keepdims=True) + norm_eps)
    normed = (x_float * radius * norm_gain).astype(jnp.bfloat16)
    pre_act = jnp.dot(normed, up_weight, preferred_element_type=jnp.float32)
    hidden = jax.nn.gelu(pre_act, approximate=False).astype(jnp.bfloat16)
    partial_out = lax.dot_general(
        hidden, down_weight, (((1,), (1,)), ((), ())), preferred_element_type=jnp.float32
    )
    summed = lax.psum_scatter(
        partial_out.astype(jnp.bfloat16), "mp", scatter_dimension=1, tiled=True
    ).astype(jnp.float32)
    col_offset = lax.axis_index("mp") * local_width
    scale_local = lax.dynamic_slice_in_dim(layer_scale, col_offset, local_width)
    x_local = local_x.reshape(total_rows, local_width).astype(jnp.float32)
    embedded = (
        ((x_local + scale_local * summed) * row_mask).astype(jnp.bfloat16).reshape(tiles.shape)
    )
    grad_out = (full_grad.reshape(total_rows, -1).astype(jnp.float32) * layer_scale).astype(
        jnp.bfloat16
    )
    grad_hidden = jnp.dot(grad_out, down_weight, preferred_element_type=jnp.float32)
    grad_pre = (grad_hidden * gelu_slope(pre_act)).astype(jnp.bfloat16)
    weight_grads = lax.psum_scatter(
        column_product(normed, grad_pre).astype(jnp.bfloat16), "dp", scatter_dimension=0, tiled=True
    )
    grad_normed = lax.dot_general(
        grad_pre, up_weight, (((1,), (1,)), ((), ())), preferred_element_type=jnp.float32
    )
    scaled = grad_normed * norm_gain
    grad_input = radius * scaled - x_float * radius * radius * radius * jnp.mean(
        scaled * x_float, axis=1, keepdims=True
    )
    grad_sum = lax.psum_scatter(
        grad_input.astype(jnp.bfloat16), "mp", scatter_dimension=1, tiled=True
    ).astype(jnp.float32)
    grad_local = local_grad.reshape(total_rows, local_width).astype(jnp.float32)
    tile_grads = ((grad_local + grad_sum) * row_mask).astype(jnp.bfloat16).reshape(tiles.shape)
    return (embedded, tile_grads, weight_grads)


def solution(mesh):
    in_specs = (
        P("dp", None, "mp"),
        P(),
        P(),
        P("dp", None, "mp"),
        P(),
        P(),
        P(None, "mp"),
        P(None, "mp"),
    )
    out_specs = (P("dp", None, "mp"), P("dp", None, "mp"), P("dp", "mp"))
    return jax.shard_map(local, mesh=mesh, in_specs=in_specs, out_specs=out_specs, check_vma=False)
```

profile of v0, /device:TPU:32, one launch (start us, length us, event | category | flops | bytes accessed | tf_op | source)
XLA Modules:
  0.0 260.8 jit_solution(17354172101906779768)
XLA Ops:
  7.2 0.8 reshape.144
  8.1 0.8 mul.143
  9.0 0.1 and_reduce_fusion
  9.1 0.2 dynamic-slice_reduce_fusion
  9.3 0.3 convolution_convert_fusion.2
  9.7 0.8 copy.109
  10.5 11.2 %all-to-all-start = ((bf16[32,8,400]{2,1,0:T(8,128)(2,1)}), bf16[32,8,400]{2,1,0:T(8,128)(2,1)S(1)}, u32[]{:S(2)}, u32[]{:S(2)}) async-start(bf16[32,8,400]{2,1,0:T(8,128)(2,1)} %copy.109), calls=%async_computation | async-start | bytes 524288 | tf_op jit(solution)/shard_map/all_to_all | solution.py:49
  21.8 0.1 copy.107
  21.9 0.1 reduce.1
  22.1 0.6 convert_reduce_fusion
  22.7 0.6 iota_compare_fusion.2
  23.4 0.8 bitcast_convert_fusion
  24.2 0.5 copy.119
  24.7 32.9 %all_gather.7 = bf16[16,8,3200]{0,1,2:T(8,128)(2,1)} all-gather(bf16[16,8,400]{0,1,2:T(8,128)(2,1)S(1)} %copy.119), channel_id=1, replica_groups=mesh['dp'=32,'mp'=8] {'mp'}, dimensions={2}, use_global_device_ids=true | all-gather | bytes 921600 | tf_op jit(solution)/shard_map/all_gather | solution.py:64
  57.6 7.4 %copy.120 = bf16[16,8,3200]{2,1,0:T(8,128)(2,1)} copy(bf16[16,8,3200]{0,1,2:T(8,128)(2,1)} %all_gather.7) | data formatting | bytes 1638400 | tf_op jit(solution)/shard_map/all_gather | solution.py:64
  65.0 0.9 fusion.96
  65.9 0.5 copy.112
  66.4 32.7 %all_gather.6 = bf16[16,8,3200]{0,1,2:T(8,128)(2,1)} all-gather(bf16[16,8,400]{0,1,2:T(8,128)(2,1)S(1)} %copy.112), channel_id=1, replica_groups=mesh['dp'=32,'mp'=8] {'mp'}, dimensions={2}, use_global_device_ids=true | all-gather | bytes 921600 | tf_op jit(solution)/shard_map/all_gather | solution.py:63
  99.1 6.6 %copy.113 = bf16[16,8,3200]{2,1,0:T(8,128)(2,1)S(1)} copy(bf16[16,8,3200]{0,1,2:T(8,128)(2,1)} %all_gather.6) | data formatting | bytes 1638400 | tf_op jit(solution)/shard_map/all_gather | solution.py:63
  105.7 0.2 fusion.1
  106.0 0.1 convert_bitcast_fusion
  106.3 0.1 rsqrt.12
  106.4 1.0 copy.116
  107.4 4.0 %fusion.95 = f32[128,800]{0,1:T(8,128)S(1)} fusion(bf16[3200,800]{0,1:T(8,128)(2,1)} %param.14, f32[128,3200]{0,1:T(8,128)S(1)} %copy.116, f32[3200]{0:T(1024)S(1)} %copy-done.4, f32[128]{0:T(128)S(1)} %rsqrt.12), kind=kOutput, calls=%fused_computation.138 | convolution fusion | flops 656588800 | bytes 7181312 | tf_op jit(solution)/shard_map/dot_general | solution.py:69
  111.5 6.4 %convolution_convert_fusion.1 = bf16[128,3200]{0,1:T(8,128)(2,1)} fusion(bf16[3200,800]{0,1:T(8,128)(2,1)} %param.15, f32[128,800]{0,1:T(8,128)S(1)} %fusion.95), kind=kOutput, calls=%fused_computation.2 | convolution fusion | flops 662425600 | bytes 6348800 | tf_op jit(solution)/shard_map/dot_general | solution.py:71
  117.9 0.2 reduce-scatter.7.cloned.1.call-start
  118.1 4.0 %fusion.3 = bf16[128,800]{0,1:T(8,128)(2,1)S(1)} fusion(bf16[3200,800]{0,1:T(8,128)(2,1)} %param.15, bf16[16,8,3200]{2,1,0:T(8,128)(2,1)S(1)} %copy-done.3, f32[3200]{0:T(1024)S(1)} %copy-done.7, f32[128,800]{0,1:T(8,128)S(1)} %fusion.95), kind=kOutput, calls=%fused_computation.13 | convolution fusion | flops 657612800 | bytes 6566400 | tf_op jit(solution)/shard_map/dot_general | solution.py:86
  122.1 4.9 %multiply_reduce_fusion = (f32[128]{0:T(128)S(1)}, f32[128,3200]{0,1:T(8,128)S(1)}) fusion(f32[128,3200]{0,1:T(8,128)S(1)} %copy.116, f32[3200]{0:T(1024)S(1)} %copy-done.4, bf16[128,800]{0,1:T(8,128)(2,1)S(1)} %fusion.3, bf16[3200,800]{0,1:T(8,128)(2,1)} %param.14), kind=kOutput, calls=%fused_computation.9 | convolution fusion | flops 656588672 | bytes 8614912 | tf_op jit(solution)/shard_map/dot_general | solution.py:91
  127.0 4.3 %convolution_convert_fusion = bf16[3200,800]{1,0:T(8,128)(2,1)} fusion(bf16[128,800]{0,1:T(8,128)(2,1)S(1)} %fusion.3, f32[128,3200]{0,1:T(8,128)S(1)} %copy.116, f32[3200]{0:T(1024)S(1)} %copy-done.4, f32[128]{0:T(128)S(1)} %rsqrt.12), kind=kOutput, calls=%fused_computation | convolution fusion | flops 659148800 | bytes 6976512 | tf_op jit(solution)/shard_map/dot_general | solution.py:19
  131.2 1.3 subtract_convert_fusion
  132.6 97.4 %fusion = bf16[112,800]{1,0:T(8,128)(2,1)S(1)} fusion(bf16[3200,800]{1,0:T(8,128)(2,1)} %convolution_convert_fusion), kind=kCustom, calls=%all-reduce-scatter | all-reduce-scatter fusion | flops 2867201 | bytes 5300224
  230.0 2.0 collective-permute-start.2
  232.1 3.9 %collective-permute-start.1 = (bf16[112,800]{1,0:T(8,128)(2,1)S(1)}, bf16[112,800]{1,0:T(8,128)(2,1)S(1)}, u32[]{:S(2)}, u32[]{:S(2)}) collective-permute-start(bf16[112,800]{1,0:T(8,128)(2,1)S(1)} %fusion), channel_id=1, source_target_pairs={{0,16},{8,24},{16,32},{24,40},{32,48},{40,56},{48,64},{56,72},{64,... | collective-permute-start | bytes 537608
  236.0 1.9 collective-permute-start
  238.0 1.5 collective-permute-start.3
  239.5 0.7 fusion.94
  240.2 0.1 convert_element_type.126
  240.3 0.1 copy.123
  240.5 0.6 dynamic-slice.4
  241.7 0.2 copy.134
  241.9 0.1 copy.117
  242.0 3.3 %collective-permute-done.1 = bf16[112,800]{1,0:T(8,128)(2,1)S(1)} collective-permute-done((bf16[112,800]{1,0:T(8,128)(2,1)S(1)}, bf16[112,800]{1,0:T(8,128)(2,1)S(1)}, u32[]{:S(2)}, u32[]{:S(2)}) %collective-permute-start.1) | collective-permute-done | bytes 179232
  245.3 3.7 %collective-permute-done = bf16[112,800]{1,0:T(8,128)(2,1)S(1)} collective-permute-done((bf16[112,800]{1,0:T(8,128)(2,1)S(1)}, bf16[112,800]{1,0:T(8,128)(2,1)S(1)}, u32[]{:S(2)}, u32[]{:S(2)}) %collective-permute-start) | collective-permute-done | bytes 179232
  249.0 1.6 concatenate
  250.7 0.7 constant_dynamic-slice_fusion
  251.4 1.1 multiply_convert_fusion.1
  252.5 0.8 copy.124
  253.2 0.8 copy.118
  (39 shorter events, 0.8 us)
Async XLA Ops:
  7.2 2.2 copy-start
  7.2 16.2 %copy-start.5 = (bf16[16,8,400]{2,1,0:T(8,128)(2,1)S(1)}, bf16[16,8,400]{2,1,0:T(8,128)(2,1)}, u32[]{:S(2)}) copy-start(bf16[16,8,400]{2,1,0:T(8,128)(2,1)} %param.11) | copy-start | bytes 307204
  10.5 54.5 %all-to-all-start = ((bf16[32,8,400]{2,1,0:T(8,128)(2,1)}), bf16[32,8,400]{2,1,0:T(8,128)(2,1)S(1)}, u32[]{:S(2)}, u32[]{:S(2)}) async-start(bf16[32,8,400]{2,1,0:T(8,128)(2,1)} %copy.109), calls=%async_computation | async-start | bytes 524288 | tf_op jit(solution)/shard_map/all_to_all | solution.py:49
  21.7 229.6 %reduce-scatter.5.cloned.1.call-start = ((), (), s32[]{:S(2)}) async-start(), calls=%async_computation.3 | async-start | bytes 921600 | tf_op jit(solution)/shard_map/reduce_scatter | solution.py:74
  106.3 1.0 copy-start.4
  111.4 6.7 %copy-start.3 = (bf16[16,8,3200]{2,1,0:T(8,128)(2,1)S(1)}, bf16[16,8,3200]{2,1,0:T(8,128)(2,1)}, u32[]{:S(2)}) copy-start(bf16[16,8,3200]{2,1,0:T(8,128)(2,1)} %copy.120) | copy-start | bytes 2457604
  111.5 6.7 %copy-start.7 = (f32[3200]{0:T(1024)S(1)}, f32[3200]{0:T(1024)}, u32[]{:S(2)}) copy-start(f32[3200]{0:T(1024)} %param.13) | copy-start | bytes 38404
  117.9 133.5 %reduce-scatter.7.cloned.1.call-start = ((), (), s32[]{:S(2)}) async-start(), calls=%async_computation.4 | async-start | bytes 921600 | tf_op jit(solution)/shard_map/reduce_scatter | solution.py:98
  132.6 107.8 %copy-start.1 = (f32[128,400]{1,0:T(8,128)S(1)}, f32[128,400]{1,0:T(8,128)}, u32[]{:S(2)}) copy-start(f32[128,400]{1,0:T(8,128)} %get-tuple-element.6) | copy-start | bytes 614404
  132.6 107.9 %copy-start.6 = (u32[256]{0:T(256)S(1)}, u32[256]{0:T(256)}, u32[]{:S(2)}) copy-start(u32[256]{0:T(256)} %constant.137) | copy-start | bytes 3076
  132.6 109.1 %copy-start.2 = (f32[16,8,400]{2,0,1:T(8,128)S(1)}, f32[16,8,400]{2,0,1:T(8,128)}, u32[]{:S(2)}) copy-start(f32[16,8,400]{2,0,1:T(8,128)} %get-tuple-element.18) | copy-start | bytes 614404
  230.0 12.0 %collective-permute-start.2 = (bf16[112,800]{1,0:T(8,128)(2,1)S(1)}, bf16[112,800]{1,0:T(8,128)(2,1)S(1)}, u32[]{:S(2)}, u32[]{:S(2)}) collective-permute-start(bf16[112,800]{1,0:T(8,128)(2,1)S(1)} %fusion), channel_id=1, source_target_pairs={{0,24},{8,32},{16,40},{24,48},{32,56},{40,64},{48,72},{56,80},{64,... | collective-permute-start | bytes 537608
  232.1 13.3 %collective-permute-start.1 = (bf16[112,800]{1,0:T(8,128)(2,1)S(1)}, bf16[112,800]{1,0:T(8,128)(2,1)S(1)}, u32[]{:S(2)}, u32[]{:S(2)}) collective-permute-start(bf16[112,800]{1,0:T(8,128)(2,1)S(1)} %fusion), channel_id=1, source_target_pairs={{0,16},{8,24},{16,32},{24,40},{32,48},{40,56},{48,64},{56,72},{64,... | collective-permute-start | bytes 537608
  236.0 13.1 %collective-permute-start = (bf16[112,800]{1,0:T(8,128)(2,1)S(1)}, bf16[112,800]{1,0:T(8,128)(2,1)S(1)}, u32[]{:S(2)}, u32[]{:S(2)}) collective-permute-start(bf16[112,800]{1,0:T(8,128)(2,1)S(1)} %fusion), channel_id=1, source_target_pairs={{0,8},{8,16},{16,24},{24,32},{32,40},{40,48},{48,56},{56,64},{64,7... | collective-permute-start | bytes 537608
  238.0 4.0 %collective-permute-start.3 = (bf16[36,800]{1,0:T(8,128)(2,1)S(1)}, bf16[36,800]{1,0:T(8,128)(2,1)S(1)}, u32[]{:S(2)}, u32[]{:S(2)}) collective-permute-start(bf16[36,800]{1,0:T(8,128)(2,1)S(1)} %slice), channel_id=1, source_target_pairs={{0,32},{8,40},{16,48},{24,56},{32,64},{40,72},{48,80},{56,88},{64,... | collective-permute-start | bytes 172808
Sparse Core Ops, SparseCore 0:
  118.0 33.7 reduce-scatter.4
  154.6 33.2 reduce-scatter.6
where the time goes:
time: 264 us; the launch traced here: 261 us
  blocking collectives  163 us (62%)
  matrix products  24.8 us (9%)
  local copies, waits for them, and re-layouts  24.4 us (9%)
  starting transfers between devices  20.8 us (8%)
  between operations  15.1 us (6%)
  waiting for transfers between devices  7.02 us (3%)
  other arithmetic  5.82 us (2%)
    unnamed x1, blocking collectives  97.4 us
    all_gather x1, blocking collectives, local(): lax.all_gather(local_grad, 'mp', axis=2, tiled=True)  32.9 us
    all_gather x1, blocking collectives, local(): lax.all_gather(local_x, 'mp', axis=2, tiled=True)  32.7 us
    all_to_all x1, starting transfers between devices, local(): lax.all_to_all(outgoing, 'dp', split_axis=0, concat_axis=0, tiled=True)  11.2 us
    unnamed x4, starting transfers between devices  9.33 us
    all_gather x1, local copies, waits for them, and re-layouts, local(): lax.all_gather(local_grad, 'mp', axis=2, tiled=True)  7.43 us
    unnamed x6, waiting for transfers between devices  7.02 us
    all_gather x1, local copies, waits for them, and re-layouts, local(): lax.all_gather(local_x, 'mp', axis=2, tiled=True)  6.64 us
  transfers between devices with their start and end apart: 7, of which 2 were waited for; matrix products, arithmetic and copies ran while one was open for 48% of the time, Pallas kernels for 0%

commit v1 on v0

v1 whole, which is shorter than its diff:
```python
import functools

import jax
import jax.numpy as jnp
from jax import lax
from jax.experimental import pallas as pl
from jax.experimental.pallas import tpu as pltpu
from jax.sharding import PartitionSpec as P

norm_eps = 1e-06
half_root = 0.7071067811865476
pdf_scale = 0.3989422804014327
RING = 4
BF = jnp.bfloat16
F32 = jnp.float32


def round_up(value, to):
    return -(-value // to) * to


def make_sizes(mesh_dp, width, ff, slots, rows):
    s = {}
    s["NZ"] = mesh_dp // RING
    s["W"] = width
    s["F"] = ff
    s["SLOTS"] = slots
    s["R"] = rows
    s["T"] = slots * rows
    s["DP"] = mesh_dp
    s["FA"] = (ff // 2) // 128 * 128
    s["FB"] = ff - s["FA"]
    s["CB"] = s["NZ"] // 2
    s["CH"] = width // s["CB"]
    s["CP"] = round_up(s["CH"], 16)
    s["XW"] = width + 16
    s["LW"] = round_up(width + 16, 128)
    return s


def first_dims(left, right):
    return lax.dot_general(left, right, (((0,), (0,)), ((), ())), preferred_element_type=F32)


def last_dims(left, right):
    return lax.dot_general(left, right, (((1,), (1,)), ((), ())), preferred_element_type=F32)


def grid_of(shape, axis):
    return lax.broadcasted_iota(jnp.int32, shape, axis)


def kernel(
    s, n_copies,
    enc, cnt, tiles, out_grad, gain, scale, up_hbm, down_hbm,
    emb_out, tg_out, wg_out,
    up_v, down_v, out1, in1, out2, in2, g_all, x_all, wide, tall, placed_v, gm_v,
    hid_v, gpr_v, acc_v, gh_v, sel_v, px, xq, gpa, gpb,
    ps_o, pr_o, sb_o, rb_o, ps_g, pr_g, sb_g, rb_g,
    zsa, zra, zsb, zrb,
    wsem, send_sem, recv_sem,
):
    NZ, W, F, SLOTS, R, T, DP = (s[k] for k in ("NZ", "W", "F", "SLOTS", "R", "T", "DP"))
    FA, FB, CB, CH, CP, XW, LW = (s[k] for k in ("FA", "FB", "CB", "CH", "CP", "XW", "LW"))
    D = W * 2 * RING
    dp = lax.axis_index("dp")
    mp = lax.axis_index("mp")
    x, z = dp // NZ, dp % NZ
    y, c = mp // 2, mp % 2
    other = 1 - c

    def at_x(k):
        return {"dp": (x + k + RING) % RING * NZ + z, "mp": mp}

    def at_z(k):
        return {"dp": x * NZ + (z + k + NZ) % NZ, "mp": mp}

    def at_y(k):
        return {"dp": dp, "mp": (y + k + RING) % RING * 2 + c}

    partner = {"dp": dp, "mp": y * 2 + other}
    used = []

    def send(src, dst, device):
        at = len(used)
        copy = pltpu.make_async_remote_copy(
            src_ref=src, dst_ref=dst, send_sem=send_sem.at[at], recv_sem=recv_sem.at[at],
            device_id=device, device_id_type=pl.DeviceIdType.MESH,
        )
        copy.start()
        used.append(copy)
        return copy

    barrier = pltpu.get_barrier_semaphore()
    peers = [at_x(k) for k in range(1, RING)] + [at_z(k) for k in range(1, NZ)]
    peers += [at_y(1), at_y(-1), partner]
    for device in peers:
        pl.semaphore_signal(barrier, inc=1, device_id=device, device_id_type=pl.DeviceIdType.MESH)

    loads = []
    for j in range(2 * RING):
        loads.append(pltpu.make_async_copy(down_hbm.at[j], down_v.at[j], wsem.at[j]))
    for j in range(2 * RING):
        loads.append(pltpu.make_async_copy(up_hbm.at[j], up_v.at[j], wsem.at[2 * RING + j]))
    for load in loads:
        load.start()

    lane = grid_of((1, T), 1)
    dest = jnp.full((1, T), -1, jnp.int32)
    for j in range(SLOTS):
        live = (j % 8) < cnt[dp * (SLOTS // 8) + j // 8]
        goes = jnp.where(live, enc[dp * SLOTS + j], -1)
        dest = jnp.where((lane // R) == j, goes, dest)
    rows_all = DP * R
    row = grid_of((rows_all, T), 0)
    slot = row // R
    target = (slot % RING) * NZ + slot // RING
    picker = (target == dest) & ((row % R) == (grid_of((rows_all, T), 1) % R))
    picked = jnp.dot(picker.astype(BF), tiles[...], preferred_element_type=F32).astype(BF)
    out1[...] = picked.reshape(NZ, RING * R, W)

    pl.semaphore_wait(barrier, len(peers))
    stage1 = [send(out1.at[(z + k) % NZ], in1.at[z], at_z(k)) for k in range(1, NZ)]
    in1[z] = out1[z]

    lane_all = grid_of((1, rows_all), 1) // R

    def look(source, carry):
        count, order = carry
        comes = jnp.int32(0)
        for j in range(SLOTS):
            live = (j % 8) < cnt[source * (SLOTS // 8) + j // 8]
            here = enc[source * SLOTS + j] == dp
            comes = comes | (here.astype(jnp.int32) * live.astype(jnp.int32))
        order = jnp.where(
            lane_all == source, jnp.where(comes > 0, count, jnp.int32(SLOTS)), order
        )
        return count + comes, order

    count, order = lax.fori_loop(
        0, DP, look, (jnp.int32(0), jnp.full((1, rows_all), SLOTS, jnp.int32))
    )
    filled = (grid_of((T, 1), 0) // R) < count

    def local_part(ref):
        part = jnp.zeros((1, W), F32)
        for j in range(2 * RING):
            part = jnp.where(mp == j, ref[:, j * W : (j + 1) * W], part)
        return part

    gain_here = local_part(gain)
    scale_here = local_part(scale)

    masked = jnp.where(filled, out_grad[...].astype(F32), 0.0)
    gm_v[...] = masked
    wide[...] = jnp.zeros_like(wide)
    wide[:, :W] = masked * scale_here
    g_all[mp] = jnp.transpose(wide[...])[:W].astype(BF)

    def gather_1(buf):
        return (
            send(buf.at[mp], buf.at[mp], at_y(1)),
            send(buf.at[mp], buf.at[mp], at_y(-1)),
            send(buf.at[mp], buf.at[mp], partner),
        )

    from_left = (y + RING - 1) % RING * 2 + c
    from_right = (y + 1) % RING * 2 + c
    from_far = (y + 2) % RING * 2 + c

    def gather_2(buf, first, half, size):
        right, left, _ = first
        right.wait_recv()
        low = pl.ds(0, half)
        high = pl.ds(half, size - half)
        far_r = send(buf.at[from_left, low], buf.at[from_left, low], at_y(1))
        share_l = send(buf.at[from_left], buf.at[from_left], partner)
        left.wait_recv()
        far_l = send(buf.at[from_right, high], buf.at[from_right, high], at_y(-1))
        share_r = send(buf.at[from_right], buf.at[from_right], partner)
        return far_r, far_l, share_l, share_r

    def gather_3(buf, second, half, size):
        far_r, far_l, _, _ = second
        low = pl.ds(0, half)
        high = pl.ds(half, size - half)
        far_r.wait_recv()
        share_a = send(buf.at[from_far, low], buf.at[from_far, low], partner)
        far_l.wait_recv()
        share_b = send(buf.at[from_far, high], buf.at[from_far, high], partner)
        return share_a, share_b

    g_half = round_up(W // 2, 16)
    x_half = round_up(XW // 2, 16)
    g_first = gather_1(g_all)

    to_row = grid_of((rows_all, rows_all), 0)
    from_row = grid_of((rows_all, rows_all), 1)
    swap_slot = to_row // R
    wants = ((swap_slot % NZ) * RING + swap_slot // NZ) * R + to_row % R
    swap = (wants == from_row).astype(BF)
    for copy in stage1:
        copy.wait_recv()
    swapped = jnp.dot(
        swap, in1[...].reshape(rows_all, W), preferred_element_type=F32
    ).astype(BF)
    out2[...] = swapped.reshape(RING, NZ * R, W)
    stage2 = [send(out2.at[(x + k) % RING], in2.at[x], at_x(k)) for k in range(1, RING)]
    in2[x] = out2[x]

    g_second = gather_2(g_all, g_first, g_half, W)

    pack_row = grid_of((T, rows_all), 0)
    packer = ((pack_row // R) == order) & (
        (pack_row % R) == (grid_of((T, rows_all), 1) % R)
    )
    packer = packer.astype(BF)
    sel_row = grid_of((CB * CP, W), 0)
    sel_col = grid_of((CB * CP, W), 1)
    sel = jnp.zeros((CB * CP, W), jnp.bool_)
    for k in range(CB):
        sel = sel | (
            (sel_row - k * CP == sel_col - k * CH)
            & (sel_row >= k * CP)
            & (sel_row < k * CP + CH)
        )
    sel_v[...] = sel.astype(BF)

    for copy in stage2:
        copy.wait_recv()
    placed = jnp.dot(packer, in2[...].reshape(rows_all, W), preferred_element_type=F32)
    placed_v[...] = placed
    squares = jnp.sum(placed * placed, axis=1, keepdims=True)
    upper = squares.astype(BF).astype(F32)
    lower = squares - upper
    wide[:, :W] = placed * gain_here
    spread = wide[...]
    wide_lane = grid_of((T, LW), 1)
    spread = jnp.where(wide_lane == W, upper, jnp.where(wide_lane == W + 1, lower, spread))
    x_all[mp] = jnp.transpose(spread)[:XW].astype(BF)
    x_first = gather_1(x_all)

    g_third = gather_3(g_all, g_second, g_half, W)
    x_second = gather_2(x_all, x_first, x_half, XW)

    for copy in (g_first[2], g_second[2], g_second[3], g_third[0], g_third[1]):
        copy.wait_recv()
    for load in loads[: 2 * RING]:
        load.wait()
    gh_v[...] = jnp.zeros_like(gh_v)

    @pl.loop(0, 2 * RING)
    def _(j):
        gh_v[...] += first_dims(g_all[j], down_v[j])

    x_third = gather_3(x_all, x_second, x_half, XW)
    for load in loads[2 * RING :]:
        load.wait()
    for copy in (x_first[2], x_second[2], x_second[3], x_third[0], x_third[1]):
        copy.wait_recv()

    def quarter(block):
        moved = jnp.dot(sel_v[...], x_all[block, :W], preferred_element_type=F32)
        return moved.astype(BF).reshape(CB, CP, T)

    mine = pl.ds(c * CB, CB)
    xq_sent = []
    for at, k in enumerate((2, 1, 3)):
        px[at] = quarter((x + k) % RING * 2 + c)
        xq_sent.append(send(px.at[at], xq.at[x, mine], at_x(k)))
    acc_v[...] = jnp.zeros_like(acc_v)

    @pl.loop(0, 2 * RING)
    def _(j):
        acc_v[...] += first_dims(x_all[j, :W], up_v[j])

    tails = jnp.zeros((16, T), F32)
    for j in range(2 * RING):
        tails = tails + x_all[j, W:XW].astype(F32)
    total = jnp.sum(tails, axis=0, keepdims=True)
    radius = lax.rsqrt(
        jnp.transpose(jnp.broadcast_to(total, (128, T)))[:, :1] / D + norm_eps
    )

    def through(lo, hi):
        raw = acc_v[:, lo:hi]
        pre = radius * raw
        cdf = 0.5 * (1.0 + lax.erf(pre * half_root))
        slope = cdf + pre * jnp.exp(-0.5 * pre * pre) * pdf_scale
        hid_v[:, lo:hi] = (pre * cdf).astype(BF)
        back = (radius * (gh_v[:, lo:hi] * slope)).astype(BF)
        gpr_v[:, lo:hi] = back
        return back, jnp.sum(back.astype(F32) * raw, axis=1, keepdims=True)

    back_a, dot_a = through(0, FA)
    gpa[x] = back_a
    ga = (send(gpa.at[x], gpa.at[x], at_x(1)), send(gpa.at[x], gpa.at[x], at_x(-1)))
    back_b, dot_b = through(FA, F)
    gpb[x] = back_b
    gb = (send(gpb.at[x], gpb.at[x], at_x(1)), send(gpb.at[x], gpb.at[x], at_x(-1)))
    dots = jnp.transpose(jnp.broadcast_to((dot_a + dot_b) / D, (T, 128)))[:16]

    def block_of(k, core):
        return (y + k + RING) % RING * 2 + core

    def out_term(k, core):
        return last_dims(down_v[block_of(k, core)], hid_v[...])

    def grad_term(k, core):
        return last_dims(up_v[block_of(k, core)], gpr_v[...])

    steps = (2, 1, -1, 0)
    pair_o, pair_g = {}, {}
    for at, k in enumerate(steps):
        ps_o[at] = out_term(k, other).astype(BF)
        pair_o[k] = (at, send(ps_o.at[at], pr_o.at[at], partner))
    for at, k in enumerate((-2, 1, -1, 0)):
        ps_g[at, :W] = grad_term(k, other).astype(BF)
        ps_g[at, W:] = dots.astype(BF)
        pair_g[k] = (at, send(ps_g.at[at], pr_g.at[at], partner))

    def out_sum(k):
        at, copy = pair_o[k]
        term = out_term(k, c)
        copy.wait_recv()
        return term + pr_o[at].astype(F32)

    def grad_sum(k):
        at, copy = pair_g[k]
        term = grad_term(k, c)
        copy.wait_recv()
        both = pr_g[at].astype(F32)
        return term + both[:W], dots + both[W:]

    sb_o[0] = out_sum(2).astype(BF)
    o_far = send(sb_o.at[0], rb_o.at[0], at_y(1))
    main, tail = grad_sum(-2)
    sb_g[0, :W] = main.astype(BF)
    sb_g[0, W:] = tail.astype(BF)
    g_far = send(sb_g.at[0], rb_g.at[0], at_y(-1))
    sb_o[1] = out_sum(-1).astype(BF)
    o_left = send(sb_o.at[1], rb_o.at[1], at_y(-1))
    main, tail = grad_sum(1)
    sb_g[1, :W] = main.astype(BF)
    sb_g[1, W:] = tail.astype(BF)
    g_right = send(sb_g.at[1], rb_g.at[1], at_y(1))

    xq_shared = []
    for at, k in enumerate((2, 1, 3)):
        source = (x - k + RING) % RING
        xq_sent[at].wait_recv()
        xq_shared.append(send(xq.at[source, mine], xq.at[source, mine], partner))
    xl, xr = (x + RING - 1) % RING, (x + 1) % RING
    ga[0].wait_recv()
    ga_far = send(gpa.at[xl], gpa.at[xl], at_x(1))
    ga[1].wait_recv()
    gb[0].wait_recv()
    gb[1].wait_recv()
    gb_far = send(gpb.at[xr], gpb.at[xr], at_x(-1))
    for core in range(2):
        xq[x, core * CB : (core + 1) * CB] = quarter(x * 2 + core)

    main = out_sum(1)
    o_far.wait_recv()
    sb_o[2] = (main + rb_o[0].astype(F32)).astype(BF)
    o_right = send(sb_o.at[2], rb_o.at[2], at_y(1))
    main, tail = grad_sum(-1)
    g_far.wait_recv()
    sb_g[2, :W] = (main + rb_g[0, :W].astype(F32)).astype(BF)
    sb_g[2, W:] = (tail + rb_g[0, W:].astype(F32)).astype(BF)
    g_left = send(sb_g.at[2], rb_g.at[2], at_y(-1))

    for copy in xq_shared:
        copy.wait_recv()

    def weight_term(k, right):
        at = (z + k + NZ) % NZ
        left = jnp.concatenate([xq[r, at] for r in range(RING)], axis=1)
        return jnp.dot(left, right[...].reshape(RING * T, -1), preferred_element_type=F32)

    half = NZ // 2
    rings = []
    for right, sbuf, rbuf, up_dir in ((gpa, zsa, zra, 1), (gpb, zsb, zrb, -1)):
        rings.append((right, sbuf, rbuf, up_dir, half, []))
        rings.append((right, sbuf, rbuf, -up_dir, half - 1, []))

    def ring_step(ring, far, at):
        right, sbuf, rbuf, way, length, sent = ring
        step = len(sent)
        if step >= length:
            return
        d = length - step
        value = weight_term(way * d, right)
        if step > 0:
            sent[-1].wait_recv()
            value = value + rbuf[at - 1].astype(F32)
        sbuf[at] = value.astype(BF)
        sent.append(send(sbuf.at[at], rbuf.at[at], at_z(way)))

    def both_ways(pair, step):
        ring_step(rings[2 * pair], None, step)
        ring_step(rings[2 * pair + 1], None, half + step)

    ga_far.wait_recv()
    both_ways(0, 0)
    gb_far.wait_recv()
    both_ways(1, 0)

    main = out_sum(0)
    o_left.wait_recv()
    o_right.wait_recv()
    tall[...] = jnp.zeros_like(tall)
    tall[:W] = main + rb_o[1].astype(F32) + rb_o[2].astype(F32)
    branch = jnp.transpose(tall[...])[:, :W]
    emb_out[...] = jnp.where(filled, placed_v[...] + scale_here * branch, 0.0).astype(BF)

    both_ways(0, 1)
    both_ways(1, 1)

    main, tail = grad_sum(0)
    g_right.wait_recv()
    g_left.wait_recv()
    tall[:W] = main + rb_g[1, :W].astype(F32) + rb_g[2, :W].astype(F32)
    tall[W:XW] = tail + rb_g[1, W:].astype(F32) + rb_g[2, W:].astype(F32)
    turned = jnp.transpose(tall[...])
    mean_dot = turned[:, W : W + 1]
    grad_in = gain_here * turned[:, :W] - placed_v[...] * (radius * radius * mean_dot)
    tg_out[...] = jnp.where(filled, gm_v[...] + grad_in, 0.0).astype(BF)

    for step in range(2, half):
        both_ways(0, step)
        both_ways(1, step)

    for pair, lo, hi in ((0, 0, FA), (1, FA, F)):
        value = weight_term(0, rings[2 * pair][0])
        for which, base in ((0, 0), (1, half)):
            _, _, rbuf, _, length, sent = rings[2 * pair + which]
            if length > 0:
                sent[-1].wait_recv()
                value = value + rbuf[base + length - 1].astype(F32)
        wg_out[:, lo:hi] = value[:CH].astype(BF)

    for copy in used:
        copy.wait_send()
    assert len(used) <= n_copies, len(used)


def local(
    tiles, tile_counts, encoder_rank, out_grad, norm_gain, layer_scale, up_weight, down_weight
):
    slots, rows, width = tiles.shape
    ff = up_weight.shape[1]
    s = make_sizes(lax.axis_size("dp"), width, ff, slots, rows)
    NZ, W, F, T, DP = (s[k] for k in ("NZ", "W", "F", "T", "DP"))
    FA, FB, CB, CH, CP, XW, LW = (s[k] for k in ("FA", "FB", "CB", "CH", "CP", "XW", "LW"))
    D = W * 2 * RING
    n_copies = 60 + 6 * NZ
    vm = pl.BlockSpec(memory_space=pltpu.VMEM)
    sm = pl.BlockSpec(memory_space=pltpu.SMEM)
    hbm = pl.BlockSpec(memory_space=pl.ANY)
    scratch = [
        pltpu.VMEM((2 * RING, W, F), BF),
        pltpu.VMEM((2 * RING, W, F), BF),
        pltpu.VMEM((NZ, RING * rows, W), BF),
        pltpu.VMEM((NZ, RING * rows, W), BF),
        pltpu.VMEM((RING, NZ * rows, W), BF),
        pltpu.VMEM((RING, NZ * rows, W), BF),
        pltpu.VMEM((2 * RING, W, T), BF),
        pltpu.VMEM((2 * RING, XW, T), BF),
        pltpu.VMEM((T, LW), F32),
        pltpu.VMEM((LW, T), F32),
        pltpu.VMEM((T, W), F32),
        pltpu.VMEM((T, W), F32),
        pltpu.VMEM((T, F), BF),
        pltpu.VMEM((T, F), BF),
        pltpu.VMEM((T, F), F32),
        pltpu.VMEM((T, F), F32),
        pltpu.VMEM((CB * CP, W), BF),
        pltpu.VMEM((RING - 1, CB, CP, T), BF),
        pltpu.VMEM((RING, 2 * CB, CP, T), BF),
        pltpu.VMEM((RING, T, FA), BF),
        pltpu.VMEM((RING, T, FB), BF),
        pltpu.VMEM((4, W, T), BF),
        pltpu.VMEM((4, W, T), BF),
        pltpu.VMEM((3, W, T), BF),
        pltpu.VMEM((3, W, T), BF),
        pltpu.VMEM((4, XW, T), BF),
        pltpu.VMEM((4, XW, T), BF),
        pltpu.VMEM((3, XW, T), BF),
        pltpu.VMEM((3, XW, T), BF),
        pltpu.VMEM((NZ, CP, FA), BF),
        pltpu.VMEM((NZ, CP, FA), BF),
        pltpu.VMEM((NZ, CP, FB), BF),
        pltpu.VMEM((NZ, CP, FB), BF),
        pltpu.SemaphoreType.DMA((4 * RING,)),
        pltpu.SemaphoreType.DMA((n_copies,)),
        pltpu.SemaphoreType.DMA((n_copies,)),
    ]
    emb, tg, wg = pl.pallas_call(
        functools.partial(kernel, s, n_copies),
        out_shape=(
            jax.ShapeDtypeStruct((T, W), BF),
            jax.ShapeDtypeStruct((T, W), BF),
            jax.ShapeDtypeStruct((CH, F), BF),
        ),
        in_specs=[sm, sm, vm, vm, vm, vm, hbm, hbm],
        out_specs=(vm, vm, vm),
        scratch_shapes=scratch,
        compiler_params=pltpu.CompilerParams(
            collective_id=0, has_side_effects=True, vmem_limit_bytes=56 * 2**20
        ),
    )(
        encoder_rank,
        tile_counts,
        tiles.reshape(T, W),
        out_grad.reshape(T, W),
        norm_gain.reshape(1, D),
        layer_scale.reshape(1, D),
        up_weight.reshape(2 * RING, W, F),
        down_weight.reshape(2 * RING, W, F),
    )
    return emb.reshape(tiles.shape), tg.reshape(tiles.shape), wg


def solution(mesh):
    in_specs = (
        P("dp", None, "mp"),
        P(),
        P(),
        P("dp", None, "mp"),
        P(),
        P(),
        P(None, "mp"),
        P(None, "mp"),
    )
    out_specs = (P("dp", None, "mp"), P("dp", None, "mp"), P("dp", "mp"))
    return jax.shard_map(local, mesh=mesh, in_specs=in_specs, out_specs=out_specs, check_vma=False)
```

time: 264 us -> 97.7 us (0.37)
  blocking collectives: 163 us -> 0 us
  Pallas kernels: 0 us -> 71.2 us
  matrix products: 24.8 us -> 0 us
  starting transfers between devices: 20.8 us -> 0 us
  between operations: 15.1 us -> 0.64 us
  waiting for transfers between devices: 7.02 us -> 0 us
  other arithmetic: 5.82 us -> 0 us
    unnamed x1 -> x0, blocking collectives: 97.4 us -> none
    pallas_call x0 -> x1, Pallas kernels: none -> 71.2 us  [local(): pl.pallas_call(functools.partial(kernel, s, n_copies), out_shape=(jax.Sha...]
    all_gather x2 -> x0, blocking collectives: 65.6 us -> none  [the longest x1 32.9 us: local(): lax.all_gather(local_grad, 'mp', axis=2, tiled=True)]
    dot_general x7 -> x0, matrix products: 24.8 us -> none  [the longest x1 6.4 us: local(): lax.dot_general(hidden, down_weight, (((1,), (1,)), ((), ())), preferred_...]
    unnamed x21 -> x5, local copies, waits for them, and re-layouts: 3.07 us -> 22.1 us
    all_gather x2 -> x0, local copies, waits for them, and re-layouts: 14.1 us -> none  [the longest x1 7.43 us: local(): lax.all_gather(local_grad, 'mp', axis=2, tiled=True)]
    all_to_all x1 -> x0, starting transfers between devices: 11.2 us -> none  [local(): lax.all_to_all(outgoing, 'dp', split_axis=0, concat_axis=0, tiled=True)]
    unnamed x4 -> x0, starting transfers between devices: 9.33 us -> none
  transfers between devices with their start and end apart: 7 -> 0, of which waited for: 2 -> 0; matrix products, arithmetic and copies ran while one was open for 48% -> 0% of each run, Pallas kernels for 0% -> 0%
where the time goes in v1:
time: 97.7 us; the launch traced here: 96.5 us
  Pallas kernels  71.2 us (73%)
  local copies, waits for them, and re-layouts  24.7 us (25%)
    pallas_call x1, Pallas kernels, local(): pl.pallas_call(functools.partial(kernel, s, n_copies), out_shape=(jax.Sha...  71.2 us
    unnamed x5, local copies, waits for them, and re-layouts  22.1 us

profile of v1, /device:TPU:32, one launch (start us, length us, event | category | flops | bytes accessed | tf_op | source)
XLA Modules:
  0.0 96.5 jit_solution(14761443313254744886)
XLA Ops:
  0.6 1.3 %reshape.32.gain = f32[1,3200]{1,0:T(1,128)} reshape(f32[3200]{0:T(1024)} %param.12) | data formatting | bytes 25600 | tf_op jit(solution)/shard_map/reshape | solution.py:517
  2.0 1.3 %reshape.33.scale = f32[1,3200]{1,0:T(1,128)} reshape(f32[3200]{0:T(1024)} %param.13) | data formatting | bytes 25600 | tf_op jit(solution)/shard_map/reshape | solution.py:518
  3.3 8.7 %copy.11 = bf16[3200,800]{1,0:T(8,128)(2,1)} copy(bf16[3200,800]{0,1:T(8,128)(2,1)} %param.14) | data formatting | bytes 10240000 | tf_op args[6]
  12.0 8.6 %copy.12 = bf16[3200,800]{1,0:T(8,128)(2,1)} copy(bf16[3200,800]{0,1:T(8,128)(2,1)} %param.15) | data formatting | bytes 10240000 | tf_op args[7]
  20.6 71.2 %shard_map.103 = (bf16[128,400]{1,0:T(8,128)(2,1)}, bf16[128,400]{1,0:T(8,128)(2,1)}, bf16[100,800]{1,0:T(8,128)(2,1)}) custom-call(s32[512]{0:T(512)} %enc.1, s32[64]{0:T(128)} %cnt.1, bf16[128,400]{1,0:T(8,128)(2,1)} %bitcast.8, bf16[128,400]{1,0:T(8,128)(2,1)} %bitcast.9, f32[1,3200]{1,0:T(1,128)} %reshape.32.gain, f32[1,3200]{1,0:T(1,128)} %reshape.33.scale, ...), custom_call_target="tpu_custom_call" | custom-call | tf_op jit(solution)/shard_map/pallas_call | solution.py:499
  91.8 1.6 %copy.16 = bf16[16,8,400]{2,1,0:T(8,128)(2,1)} copy(bf16[16,8,400]{2,1,0:T(8,128)(2,1)} %bitcast.11) | data formatting | bytes 204800
  93.4 1.6 %copy.17 = bf16[16,8,400]{2,1,0:T(8,128)(2,1)} copy(bf16[16,8,400]{2,1,0:T(8,128)(2,1)} %bitcast.10) | data formatting | bytes 204800
  94.9 1.6 %copy.18 = bf16[100,800]{1,0:T(8,128)(2,1)} copy(bf16[100,800]{1,0:T(8,128)(2,1)} %get-tuple-element.14) | data formatting | bytes 320000

commit v2 on v1

--- a/solution.py
+++ b/solution.py
@@ -52,13 +52,14 @@
 
 def kernel(
     s, n_copies,
-    enc, cnt, tiles, out_grad, gain, scale, up_hbm, down_hbm,
+    enc, cnt, tiles_hbm, grad_hbm, gain, scale, up_hbm, down_hbm,
     emb_out, tg_out, wg_out,
-    up_v, down_v, out1, in1, out2, in2, g_all, x_all, wide, tall, placed_v, gm_v,
-    hid_v, gpr_v, acc_v, gh_v, sel_v, px, xq, gpa, gpb,
+    up_v, down_v, tiles, out_grad, emb_v, tg_v, wg_v,
+    out1, in1, out2, in2, g_all, x_all, sq_pair, sq_ring, wide, tall, placed_v, gm_v,
+    hid_v, gpr_v, acc_v, gh_v, out_t, grad_t, sel_v, px, xq, gpa, gpb,
     ps_o, pr_o, sb_o, rb_o, ps_g, pr_g, sb_g, rb_g,
     zsa, zra, zsb, zrb,
-    wsem, send_sem, recv_sem,
+    wsem, osem, send_sem, recv_sem,
 ):
     NZ, W, F, SLOTS, R, T, DP = (s[k] for k in ("NZ", "W", "F", "SLOTS", "R", "T", "DP"))
     FA, FB, CB, CH, CP, XW, LW = (s[k] for k in ("FA", "FB", "CB", "CH", "CP", "XW", "LW"))
@@ -93,17 +94,24 @@
 
     barrier = pltpu.get_barrier_semaphore()
     peers = [at_x(k) for k in range(1, RING)] + [at_z(k) for k in range(1, NZ)]
-    peers += [at_y(1), at_y(-1), partner]
+    peers += [at_y(1), at_y(2), at_y(3), partner]
     for device in peers:
         pl.semaphore_signal(barrier, inc=1, device_id=device, device_id_type=pl.DeviceIdType.MESH)
 
-    loads = []
-    for j in range(2 * RING):
-        loads.append(pltpu.make_async_copy(down_hbm.at[j], down_v.at[j], wsem.at[j]))
-    for j in range(2 * RING):
-        loads.append(pltpu.make_async_copy(up_hbm.at[j], up_v.at[j], wsem.at[2 * RING + j]))
-    for load in loads:
-        load.start()
+    first = pltpu.make_async_copy(tiles_hbm, tiles, wsem.at[0])
+    first.start()
+    second = pltpu.make_async_copy(grad_hbm, out_grad, wsem.at[1])
+    second.start()
+    load_down = pltpu.make_async_copy(down_hbm, down_v, wsem.at[2])
+    load_down.start()
+    load_up = pltpu.make_async_copy(up_hbm, up_v, wsem.at[3])
+    load_up.start()
+
+    def block(j):
+        return pl.ds(pl.multiple_of(j * W, 16), W)
+
+    def part(j, lo, size):
+        return pl.ds(pl.multiple_of(j * W + lo, 16), size)
 
     lane = grid_of((1, T), 1)
     dest = jnp.full((1, T), -1, jnp.int32)
@@ -116,6 +124,7 @@
     slot = row // R
     target = (slot % RING) * NZ + slot // RING
     picker = (target == dest) & ((row % R) == (grid_of((rows_all, T), 1) % R))
+    first.wait()
     picked = jnp.dot(picker.astype(BF), tiles[...], preferred_element_type=F32).astype(BF)
     out1[...] = picked.reshape(NZ, RING * R, W)
 
@@ -143,55 +152,55 @@
     filled = (grid_of((T, 1), 0) // R) < count
 
     def local_part(ref):
+        whole = ref[...].reshape(1, D)
         part = jnp.zeros((1, W), F32)
         for j in range(2 * RING):
-            part = jnp.where(mp == j, ref[:, j * W : (j + 1) * W], part)
+            part = jnp.where(mp == j, whole[:, j * W : (j + 1) * W], part)
         return part
 
     gain_here = local_part(gain)
     scale_here = local_part(scale)
 
+    second.wait()
     masked = jnp.where(filled, out_grad[...].astype(F32), 0.0)
     gm_v[...] = masked
     wide[...] = jnp.zeros_like(wide)
     wide[:, :W] = masked * scale_here
-    g_all[mp] = jnp.transpose(wide[...])[:W].astype(BF)
+    g_all[block(mp)] = jnp.transpose(wide[...])[:W].astype(BF)
 
     def gather_1(buf):
-        return (
-            send(buf.at[mp], buf.at[mp], at_y(1)),
-            send(buf.at[mp], buf.at[mp], at_y(-1)),
-            send(buf.at[mp], buf.at[mp], partner),
-        )
+        own = buf.at[block(mp)]
+        return send(own, own, at_y(1)), send(own, own, at_y(-1)), send(own, own, partner)
 
     from_left = (y + RING - 1) % RING * 2 + c
     from_right = (y + 1) % RING * 2 + c
     from_far = (y + 2) % RING * 2 + c
-
-    def gather_2(buf, first, half, size):
+    low = round_up(W // 2, 16)
+
+    def gather_2(buf, first):
         right, left, _ = first
         right.wait_recv()
-        low = pl.ds(0, half)
-        high = pl.ds(half, size - half)
-        far_r = send(buf.at[from_left, low], buf.at[from_left, low], at_y(1))
-        share_l = send(buf.at[from_left], buf.at[from_left], partner)
+        piece = buf.at[part(from_left, 0, low)]
+        far_r = send(piece, piece, at_y(1))
+        piece = buf.at[block(from_left)]
+        share_l = send(piece, piece, partner)
         left.wait_recv()
-        far_l = send(buf.at[from_right, high], buf.at[from_right, high], at_y(-1))
-        share_r = send(buf.at[from_right], buf.at[from_right], partner)
+        piece = buf.at[part(from_right, low, W - low)]
+        far_l = send(piece, piece, at_y(-1))
+        piece = buf.at[block(from_right)]
+        share_r = send(piece, piece, partner)
         return far_r, far_l, share_l, share_r
 
-    def gather_3(buf, second, half, size):
+    def gather_3(buf, second):
         far_r, far_l, _, _ = second
-        low = pl.ds(0, half)
-        high = pl.ds(half, size - half)
         far_r.wait_recv()
-        share_a = send(buf.at[from_far, low], buf.at[from_far, low], partner)
+        piece = buf.at[part(from_far, 0, low)]
+        share_a = send(piece, piece, partner)
         far_l.wait_recv()
-        share_b = send(buf.at[from_far, high], buf.at[from_far, high], partner)
+        piece = buf.at[part(from_far, low, W - low)]
+        share_b = send(piece, piece, partner)
         return share_a, share_b
 
-    g_half = round_up(W // 2, 16)
-    x_half = round_up(XW // 2, 16)
     g_first = gather_1(g_all)
 
     to_row = grid_of((rows_all, rows_all), 0)
@@ -208,7 +217,7 @@
     stage2 = [send(out2.at[(x + k) % RING], in2.at[x], at_x(k)) for k in range(1, RING)]
     in2[x] = out2[x]
 
-    g_second = gather_2(g_all, g_first, g_half, W)
+    g_second = gather_2(g_all, g_first)
 
     pack_row = grid_of((T, rows_all), 0)
     packer = ((pack_row // R) == order) & (
@@ -230,37 +239,32 @@
         copy.wait_recv()
     placed = jnp.dot(packer, in2[...].reshape(rows_all, W), preferred_element_type=F32)
     placed_v[...] = placed
-    squares = jnp.sum(placed * placed, axis=1, keepdims=True)
-    upper = squares.astype(BF).astype(F32)
-    lower = squares - upper
     wide[:, :W] = placed * gain_here
-    spread = wide[...]
-    wide_lane = grid_of((T, LW), 1)
-    spread = jnp.where(wide_lane == W, upper, jnp.where(wide_lane == W + 1, lower, spread))
-    x_all[mp] = jnp.transpose(spread)[:XW].astype(BF)
+    x_all[block(mp)] = jnp.transpose(wide[...])[:W].astype(BF)
     x_first = gather_1(x_all)
-
-    g_third = gather_3(g_all, g_second, g_half, W)
-    x_second = gather_2(x_all, x_first, x_half, XW)
+    wide[:, :W] = placed * placed
+    squares = jnp.sum(jnp.transpose(wide[...]), axis=0, keepdims=True)
+    sq_pair[0] = jnp.broadcast_to(squares, (8, T))
+    sq_sent = send(sq_pair.at[0], sq_pair.at[1], partner)
+
+    g_third = gather_3(g_all, g_second)
+    sq_sent.wait_recv()
+    sq_ring[0] = sq_pair[0] + sq_pair[1]
+    sq_parts = [send(sq_ring.at[0], sq_ring.at[k], at_y(k)) for k in range(1, RING)]
+    x_second = gather_2(x_all, x_first)
 
     for copy in (g_first[2], g_second[2], g_second[3], g_third[0], g_third[1]):
         copy.wait_recv()
-    for load in loads[: 2 * RING]:
-        load.wait()
-    gh_v[...] = jnp.zeros_like(gh_v)
-
-    @pl.loop(0, 2 * RING)
-    def _(j):
-        gh_v[...] += first_dims(g_all[j], down_v[j])
-
-    x_third = gather_3(x_all, x_second, x_half, XW)
-    for load in loads[2 * RING :]:
-        load.wait()
+    load_down.wait()
+    gh_v[...] = jnp.dot(down_v[...], g_all[...], preferred_element_type=F32)
+
+    x_third = gather_3(x_all, x_second)
+    load_up.wait()
     for copy in (x_first[2], x_second[2], x_second[3], x_third[0], x_third[1]):
         copy.wait_recv()
 
-    def quarter(block):
-        moved = jnp.dot(sel_v[...], x_all[block, :W], preferred_element_type=F32)
+    def quarter(j):
+        moved = jnp.dot(sel_v[...], x_all[block(j)], preferred_element_type=F32)
         return moved.astype(BF).reshape(CB, CP, T)
 
     mine = pl.ds(c * CB, CB)
@@ -268,29 +272,22 @@
     for at, k in enumerate((2, 1, 3)):
         px[at] = quarter((x + k) % RING * 2 + c)
         xq_sent.append(send(px.at[at], xq.at[x, mine], at_x(k)))
-    acc_v[...] = jnp.zeros_like(acc_v)
-
-    @pl.loop(0, 2 * RING)
-    def _(j):
-        acc_v[...] += first_dims(x_all[j, :W], up_v[j])
-
-    tails = jnp.zeros((16, T), F32)
-    for j in range(2 * RING):
-        tails = tails + x_all[j, W:XW].astype(F32)
-    total = jnp.sum(tails, axis=0, keepdims=True)
-    radius = lax.rsqrt(
-        jnp.transpose(jnp.broadcast_to(total, (128, T)))[:, :1] / D + norm_eps
-    )
+    acc_v[...] = jnp.dot(up_v[...], x_all[...], preferred_element_type=F32)
+
+    for copy in sq_parts:
+        copy.wait_recv()
+    total = sq_ring[0] + sq_ring[1] + sq_ring[2] + sq_ring[3]
+    radius = lax.rsqrt(total[:1] / D + norm_eps)
 
     def through(lo, hi):
-        raw = acc_v[:, lo:hi]
+        raw = acc_v[lo:hi]
         pre = radius * raw
         cdf = 0.5 * (1.0 + lax.erf(pre * half_root))
         slope = cdf + pre * jnp.exp(-0.5 * pre * pre) * pdf_scale
-        hid_v[:, lo:hi] = (pre * cdf).astype(BF)
-        back = (radius * (gh_v[:, lo:hi] * slope)).astype(BF)
-        gpr_v[:, lo:hi] = back
-        return back, jnp.sum(back.astype(F32) * raw, axis=1, keepdims=True)
+        acc_v[lo:hi] = pre * cdf
+        back = radius * (gh_v[lo:hi] * slope)
+        gh_v[lo:hi] = back
+        return back.astype(BF), jnp.sum(back * raw, axis=0, keepdims=True)
 
     back_a, dot_a = through(0, FA)
     gpa[x] = back_a
@@ -298,16 +295,42 @@
     back_b, dot_b = through(FA, F)
     gpb[x] = back_b
     gb = (send(gpb.at[x], gpb.at[x], at_x(1)), send(gpb.at[x], gpb.at[x], at_x(-1)))
-    dots = jnp.transpose(jnp.broadcast_to((dot_a + dot_b) / D, (T, 128)))[:16]
+    dots = jnp.broadcast_to((dot_a + dot_b) / D, (16, T))
+
+    def turn_rows(ref):
+        whole = ref[: F // 128 * 128]
+        parts = [jnp.transpose(whole)]
+        if F % 128:
+            last = jnp.concatenate([ref[F // 128 * 128 :], jnp.zeros((128 - F % 128, T), F32)], axis=0)
+            parts.append(jnp.transpose(last))
+        return jnp.concatenate(parts, axis=1)[:, :F].astype(BF)
+
+    tile = D // 5 if D % 640 == 0 else 128
+
+    hid_v[...] = turn_rows(acc_v)
+
+    @pl.loop(0, D // tile)
+    def _(t):
+        cols = pl.ds(pl.multiple_of(t * tile, 128), tile)
+        some = jnp.dot(hid_v[...], down_v[:, cols], preferred_element_type=F32)
+        out_t[cols] = jnp.transpose(some)
+
+    gpr_v[...] = turn_rows(gh_v)
+
+    @pl.loop(0, D // tile)
+    def _(t):
+        cols = pl.ds(pl.multiple_of(t * tile, 128), tile)
+        some = jnp.dot(gpr_v[...], up_v[:, cols], preferred_element_type=F32)
+        grad_t[cols] = jnp.transpose(some)
 
     def block_of(k, core):
         return (y + k + RING) % RING * 2 + core
 
     def out_term(k, core):
-        return last_dims(down_v[block_of(k, core)], hid_v[...])
+        return out_t[block(block_of(k, core))]
 
     def grad_term(k, core):
-        return last_dims(up_v[block_of(k, core)], gpr_v[...])
+        return grad_t[block(block_of(k, core))]
 
     steps = (2, 1, -1, 0)
     pair_o, pair_g = {}, {}
@@ -376,7 +399,8 @@
     def weight_term(k, right):
         at = (z + k + NZ) % NZ
         left = jnp.concatenate([xq[r, at] for r in range(RING)], axis=1)
-        return jnp.dot(left, right[...].reshape(RING * T, -1), preferred_element_type=F32)
+        turned = jnp.concatenate([right[r] for r in range(RING)], axis=1)
+        return last_dims(left, turned)
 
     half = NZ // 2
     rings = []
@@ -412,7 +436,9 @@
     tall[...] = jnp.zeros_like(tall)
     tall[:W] = main + rb_o[1].astype(F32) + rb_o[2].astype(F32)
     branch = jnp.transpose(tall[...])[:, :W]
-    emb_out[...] = jnp.where(filled, placed_v[...] + scale_here * branch, 0.0).astype(BF)
+    emb_v[...] = jnp.where(filled, placed_v[...] + scale_here * branch, 0.0).astype(BF)
+    store_emb = pltpu.make_async_copy(emb_v, emb_out, osem.at[0])
+    store_emb.start()
 
     both_ways(0, 1)
     both_ways(1, 1)
@@ -421,11 +447,14 @@
     g_right.wait_recv()
     g_left.wait_recv()
     tall[:W] = main + rb_g[1, :W].astype(F32) + rb_g[2, :W].astype(F32)
-    tall[W:XW] = tail + rb_g[1, W:].astype(F32) + rb_g[2, W:].astype(F32)
+    tail = tail + rb_g[1, W:].astype(F32) + rb_g[2, W:].astype(F32)
+    tall[W:XW] = tail * (radius * radius)
     turned = jnp.transpose(tall[...])
     mean_dot = turned[:, W : W + 1]
-    grad_in = gain_here * turned[:, :W] - placed_v[...] * (radius * radius * mean_dot)
-    tg_out[...] = jnp.where(filled, gm_v[...] + grad_in, 0.0).astype(BF)
+    grad_in = gain_here * turned[:, :W] - placed_v[...] * mean_dot
+    tg_v[...] = jnp.where(filled, gm_v[...] + grad_in, 0.0).astype(BF)
+    store_tg = pltpu.make_async_copy(tg_v, tg_out, osem.at[1])
+    store_tg.start()
 
     for step in range(2, half):
         both_ways(0, step)
@@ -438,11 +467,38 @@
             if length > 0:
                 sent[-1].wait_recv()
                 value = value + rbuf[base + length - 1].astype(F32)
-        wg_out[:, lo:hi] = value[:CH].astype(BF)
+        wg_v[:, lo:hi] = value[:CH].astype(BF)
+    store_wg = pltpu.make_async_copy(wg_v, wg_out, osem.at[2])
+    store_wg.start()
 
     for copy in used:
         copy.wait_send()
+    store_emb.wait()
+    store_tg.wait()
+    store_wg.wait()
     assert len(used) <= n_copies, len(used)
+
+
+def hand_over_kernel(a, b, c, a_out, b_out, c_out, sem):
+    copies = [
+        pltpu.make_async_copy(src, dst, sem.at[at])
+        for at, (src, dst) in enumerate(((a, a_out), (b, b_out), (c, c_out)))
+    ]
+    for copy in copies:
+        copy.start()
+    for copy in copies:
+        copy.wait()
+
+
+def hand_over(*arrays):
+    hbm = pl.BlockSpec(memory_space=pl.ANY)
+    return pl.pallas_call(
+        hand_over_kernel,
+        out_shape=tuple(jax.ShapeDtypeStruct(a.shape, a.dtype) for a in arrays),
+        in_specs=[hbm] * 3,
+        out_specs=(hbm,) * 3,
+        scratch_shapes=[pltpu.SemaphoreType.DMA((3,))],
+    )(*arrays)
 
 
 def local(
@@ -459,27 +515,36 @@
     sm = pl.BlockSpec(memory_space=pltpu.SMEM)
     hbm = pl.BlockSpec(memory_space=pl.ANY)
     scratch = [
-        pltpu.VMEM((2 * RING, W, F), BF),
-        pltpu.VMEM((2 * RING, W, F), BF),
+        pltpu.VMEM((F, D), BF),
+        pltpu.VMEM((F, D), BF),
+        pltpu.VMEM((T, W), BF),
+        pltpu.VMEM((T, W), BF),
+        pltpu.VMEM((T, W), BF),
+        pltpu.VMEM((T, W), BF),
+        pltpu.VMEM((CH, F), BF),
         pltpu.VMEM((NZ, RING * rows, W), BF),
         pltpu.VMEM((NZ, RING * rows, W), BF),
         pltpu.VMEM((RING, NZ * rows, W), BF),
         pltpu.VMEM((RING, NZ * rows, W), BF),
-        pltpu.VMEM((2 * RING, W, T), BF),
-        pltpu.VMEM((2 * RING, XW, T), BF),
+        pltpu.VMEM((D, T), BF),
+        pltpu.VMEM((D, T), BF),
+        pltpu.VMEM((2, 8, T), F32),
+        pltpu.VMEM((RING, 8, T), F32),
         pltpu.VMEM((T, LW), F32),
         pltpu.VMEM((LW, T), F32),
         pltpu.VMEM((T, W), F32),
         pltpu.VMEM((T, W), F32),
         pltpu.VMEM((T, F), BF),
         pltpu.VMEM((T, F), BF),
-        pltpu.VMEM((T, F), F32),
-        pltpu.VMEM((T, F), F32),
+        pltpu.VMEM((F, T), F32),
+        pltpu.VMEM((F, T), F32),
+        pltpu.VMEM((D, T), F32),
+        pltpu.VMEM((D, T), F32),
         pltpu.VMEM((CB * CP, W), BF),
         pltpu.VMEM((RING - 1, CB, CP, T), BF),
         pltpu.VMEM((RING, 2 * CB, CP, T), BF),
-        pltpu.VMEM((RING, T, FA), BF),
-        pltpu.VMEM((RING, T, FB), BF),
+        pltpu.VMEM((RING, FA, T), BF),
+        pltpu.VMEM((RING, FB, T), BF),
         pltpu.VMEM((4, W, T), BF),
         pltpu.VMEM((4, W, T), BF),
         pltpu.VMEM((3, W, T), BF),
@@ -492,7 +557,8 @@
         pltpu.VMEM((NZ, CP, FA), BF),
         pltpu.VMEM((NZ, CP, FB), BF),
         pltpu.VMEM((NZ, CP, FB), BF),
-        pltpu.SemaphoreType.DMA((4 * RING,)),
+        pltpu.SemaphoreType.DMA((4,)),
+        pltpu.SemaphoreType.DMA((3,)),
         pltpu.SemaphoreType.DMA((n_copies,)),
         pltpu.SemaphoreType.DMA((n_copies,)),
     ]
@@ -503,8 +569,8 @@
             jax.ShapeDtypeStruct((T, W), BF),
             jax.ShapeDtypeStruct((CH, F), BF),
         ),
-        in_specs=[sm, sm, vm, vm, vm, vm, hbm, hbm],
-        out_specs=(vm, vm, vm),
+        in_specs=[sm, sm, hbm, hbm, vm, vm, hbm, hbm],
+        out_specs=(hbm, hbm, hbm),
         scratch_shapes=scratch,
         compiler_params=pltpu.CompilerParams(
             collective_id=0, has_side_effects=True, vmem_limit_bytes=56 * 2**20
@@ -514,11 +580,12 @@
         tile_counts,
         tiles.reshape(T, W),
         out_grad.reshape(T, W),
-        norm_gain.reshape(1, D),
-        layer_scale.reshape(1, D),
-        up_weight.reshape(2 * RING, W, F),
-        down_weight.reshape(2 * RING, W, F),
+        norm_gain,
+        layer_scale,
+        up_weight.T,
+        down_weight.T,
     )
+    emb, tg, wg = hand_over(emb, tg, wg)
     return emb.reshape(tiles.shape), tg.reshape(tiles.shape), wg
 
 

time: 97.7 us -> 87.2 us (0.89)
  local copies, waits for them, and re-layouts: 24.7 us -> 0 us
  Pallas kernels: 71.2 us -> 86.3 us
    unnamed x5 -> x0, local copies, waits for them, and re-layouts: 22.1 us -> none
    pallas_call x0 -> x1, Pallas kernels: none -> 14.7 us  [hand_over(): pl.pallas_call(hand_over_kernel, out_shape=tuple((jax.ShapeDtypeStruct(a....]
    reshape x2 -> x0, local copies, waits for them, and re-layouts: 2.65 us -> none  [the longest x1 1.33 us: local(): norm_gain.reshape(1, D)]
where the time goes in v2:
time: 87.2 us; the launch traced here: 87 us
  Pallas kernels  86.3 us (99%)
    pallas_call x1, Pallas kernels, local(): pl.pallas_call(functools.partial(kernel, s, n_copies), out_shape=(jax.Sha...  71.6 us
    pallas_call x1, Pallas kernels, hand_over(): pl.pallas_call(hand_over_kernel, out_shape=tuple((jax.ShapeDtypeStruct(a....  14.7 us

profile of v2, /device:TPU:32, one launch (start us, length us, event | category | flops | bytes accessed | tf_op | source)
XLA Modules:
  0.0 87.0 jit_solution(8758816957154231200)
XLA Ops:
  0.6 71.6 %shard_map.103 = (bf16[128,400]{1,0:T(8,128)(2,1)}, bf16[128,400]{1,0:T(8,128)(2,1)}, bf16[100,800]{1,0:T(8,128)(2,1)}) custom-call(s32[512]{0:T(512)} %enc.1, s32[64]{0:T(128)} %cnt.1, bf16[128,400]{1,0:T(8,128)(2,1)} %bitcast.8, bf16[128,400]{1,0:T(8,128)(2,1)} %bitcast.9, f32[3200]{0:T(1024)} %gain.1, f32[3200]{0:T(1024)} %scale.1, ...), custom_call_target="tpu_custom_call" | custom-call | tf_op jit(solution)/shard_map/pallas_call | solution.py:565
  72.3 14.7 %shard_map.104 = (bf16[128,400]{1,0:T(8,128)(2,1)}, bf16[128,400]{1,0:T(8,128)(2,1)}, bf16[100,800]{1,0:T(8,128)(2,1)}) custom-call(bf16[128,400]{1,0:T(8,128)(2,1)} %get-tuple-element.9.a, bf16[128,400]{1,0:T(8,128)(2,1)} %get-tuple-element.10.b, bf16[100,800]{1,0:T(8,128)(2,1)} %get-tuple-element.11.c), custom_call_target="tpu_custom_call" | custom-call | tf_op jit(solution)/shard_map/pallas_call | solution.py:495

commit v3 on v2

v3 whole, which is shorter than its diff:
```python
import functools

import jax
import jax.numpy as jnp
from jax import lax
from jax.experimental import pallas as pl
from jax.experimental.pallas import tpu as pltpu
from jax.sharding import PartitionSpec as P

norm_eps = 1e-06
half_root = 0.7071067811865476
pdf_scale = 0.3989422804014327
RING = 4
BF = jnp.bfloat16
F32 = jnp.float32


def round_up(value, to):
    return -(-value // to) * to


def make_sizes(mesh_dp, width, ff, slots, rows):
    s = {}
    s["NZ"] = mesh_dp // RING
    s["W"] = width
    s["F"] = ff
    s["SLOTS"] = slots
    s["R"] = rows
    s["T"] = slots * rows
    s["DP"] = mesh_dp
    s["FP"] = ff // 3 // 128 * 128
    s["FL"] = ff - 3 * s["FP"]
    s["CB"] = s["NZ"] // 2
    s["CH"] = width // s["CB"]
    s["CP"] = round_up(s["CH"], 8)
    s["XW"] = width + 16
    s["LW"] = round_up(width + 16, 128)
    return s


def first_dims(left, right):
    return lax.dot_general(left, right, (((0,), (0,)), ((), ())), preferred_element_type=F32)


def last_dims(left, right):
    return lax.dot_general(left, right, (((1,), (1,)), ((), ())), preferred_element_type=F32)


def grid_of(shape, axis):
    return lax.broadcasted_iota(jnp.int32, shape, axis)


def kernel(
    s, n_copies,
    enc, cnt, tiles_hbm, grad_hbm, gain, scale, up_hbm, down_hbm,
    emb_out, tg_out, wg_out,
    up_v, down_v, tiles, out_grad, emb_v, tg_v, wg_v,
    out1, in1, g_all, x_all, sq_pair, sq_ring, wide, tall, placed_v, gm_v,
    hid_v, gpr_v, gh_v, out_t, grad_t, sel_v, px, xq, gp0, gp1, gp2,
    ps_o, pr_o, sb_o, rb_o, ps_g, pr_g, sb_g, rb_g,
    zs0, zr0, zs1, zr1, zs2, zr2, zs3, zr3,
    wsem, osem, send_sem, recv_sem,
):
    NZ, W, F, SLOTS, R, T, DP = (s[k] for k in ("NZ", "W", "F", "SLOTS", "R", "T", "DP"))
    FP, FL, CB, CH, CP, XW, LW = (s[k] for k in ("FP", "FL", "CB", "CH", "CP", "XW", "LW"))
    D = W * 2 * RING
    dp = lax.axis_index("dp")
    mp = lax.axis_index("mp")
    x, z = dp // NZ, dp % NZ
    y, c = mp // 2, mp % 2
    other = 1 - c

    def at_x(k):
        return {"dp": (x + k + RING) % RING * NZ + z, "mp": mp}

    def at_z(k):
        return {"dp": x * NZ + (z + k + NZ) % NZ, "mp": mp}

    def at_xz(i, k):
        return {"dp": (x + i) % RING * NZ + (z + k) % NZ, "mp": mp}

    def at_y(k):
        return {"dp": dp, "mp": (y + k + RING) % RING * 2 + c}

    partner = {"dp": dp, "mp": y * 2 + other}
    used = []

    def send(src, dst, device):
        at = len(used)
        copy = pltpu.make_async_remote_copy(
            src_ref=src, dst_ref=dst, send_sem=send_sem.at[at], recv_sem=recv_sem.at[at],
            device_id=device, device_id_type=pl.DeviceIdType.MESH,
        )
        copy.start()
        used.append(copy)
        return copy

    barrier = pltpu.get_barrier_semaphore()
    others = [(i, k) for k in range(NZ) for i in range(RING) if (i, k) != (0, 0)]
    others.sort(key=lambda ik: -min(ik[0], RING - ik[0]) - min(ik[1], NZ - ik[1]))
    peers = [at_xz(i, k) for i, k in others]
    peers += [at_y(1), at_y(2), at_y(3), partner]
    for device in peers:
        pl.semaphore_signal(barrier, inc=1, device_id=device, device_id_type=pl.DeviceIdType.MESH)

    first = pltpu.make_async_copy(tiles_hbm, tiles, wsem.at[0])
    first.start()
    second = pltpu.make_async_copy(grad_hbm, out_grad, wsem.at[1])
    second.start()
    load_down = pltpu.make_async_copy(down_hbm, down_v, wsem.at[2])
    load_down.start()
    load_up = pltpu.make_async_copy(up_hbm, up_v, wsem.at[3])
    load_up.start()

    def block(j):
        return pl.ds(pl.multiple_of(j * W, 16), W)

    def part(j, lo, size):
        return pl.ds(pl.multiple_of(j * W + lo, 16), size)

    lane = grid_of((1, T), 1)
    dest = jnp.full((1, T), -1, jnp.int32)
    for j in range(SLOTS):
        live = (j % 8) < cnt[dp * (SLOTS // 8) + j // 8]
        goes = jnp.where(live, enc[dp * SLOTS + j], -1)
        dest = jnp.where((lane // R) == j, goes, dest)
    rows_all = DP * R
    row = grid_of((rows_all, T), 0)
    picker = ((row // R) == dest) & ((row % R) == (grid_of((rows_all, T), 1) % R))
    first.wait()
    picked = jnp.dot(picker.astype(BF), tiles[...], preferred_element_type=F32)
    out1[...] = picked.reshape(DP, R, W).astype(BF)

    pl.semaphore_wait(barrier, len(peers))
    exchange = []
    for i, k in others:
        there = (x + i) % RING * NZ + (z + k) % NZ
        exchange.append(send(out1.at[there], in1.at[dp], at_xz(i, k)))
    in1[dp] = out1[dp]

    lane_all = grid_of((1, rows_all), 1) // R

    def look(source, carry):
        count, order = carry
        comes = jnp.int32(0)
        for j in range(SLOTS):
            live = (j % 8) < cnt[source * (SLOTS // 8) + j // 8]
            here = enc[source * SLOTS + j] == dp
            comes = comes | (here.astype(jnp.int32) * live.astype(jnp.int32))
        order = jnp.where(
            lane_all == source, jnp.where(comes > 0, count, jnp.int32(SLOTS)), order
        )
        return count + comes, order

    count, order = lax.fori_loop(
        0, DP, look, (jnp.int32(0), jnp.full((1, rows_all), SLOTS, jnp.int32))
    )
    filled = (grid_of((T, 1), 0) // R) < count

    def local_part(ref):
        whole = ref[...].reshape(1, D)
        part = jnp.zeros((1, W), F32)
        for j in range(2 * RING):
            part = jnp.where(mp == j, whole[:, j * W : (j + 1) * W], part)
        return part

    gain_here = local_part(gain)
    scale_here = local_part(scale)

    second.wait()
    masked = jnp.where(filled, out_grad[...].astype(F32), 0.0)
    gm_v[...] = masked
    wide[...] = jnp.zeros_like(wide)
    wide[:, :W] = masked * scale_here
    g_all[block(mp)] = jnp.transpose(wide[...])[:W].astype(BF)

    ways = (2, 1, 3)

    def gather_1(buf):
        own = buf.at[block(mp)]
        return [send(own, own, partner)] + [send(own, own, at_y(k)) for k in ways]

    def gather_2(buf, copy, k):
        copy.wait_recv()
        piece = buf.at[block((y - k + RING) % RING * 2 + c)]
        return send(piece, piece, partner)

    g_first = gather_1(g_all)

    pack_row = grid_of((T, rows_all), 0)
    packer = ((pack_row // R) == order) & (
        (pack_row % R) == (grid_of((T, rows_all), 1) % R)
    )
    packer = packer.astype(BF)
    sel_row = grid_of((CB * CP, W), 0)
    sel_col = grid_of((CB * CP, W), 1)
    sel = jnp.zeros((CB * CP, W), jnp.bool_)
    for k in range(CB):
        sel = sel | (
            (sel_row - k * CP == sel_col - k * CH)
            & (sel_row >= k * CP)
            & (sel_row < k * CP + CH)
        )
    sel_v[...] = sel.astype(BF)

    for copy in exchange:
        copy.wait_recv()
    arrived = in1[...].astype(F32).reshape(rows_all, W).astype(BF)
    placed = jnp.dot(packer, arrived, preferred_element_type=F32)
    placed_v[...] = placed
    wide[:, :W] = placed * gain_here
    x_all[block(mp)] = jnp.transpose(wide[...])[:W].astype(BF)
    x_first = gather_1(x_all)
    wide[:, :W] = placed * placed
    squares = jnp.sum(jnp.transpose(wide[...]), axis=0, keepdims=True)
    sq_pair[0] = jnp.broadcast_to(squares, (8, T))
    sq_sent = send(sq_pair.at[0], sq_pair.at[1], partner)

    mine = pl.ds(c * CB, CB)
    theirs = pl.ds(other * CB, CB)

    def quarter(j):
        moved = jnp.dot(sel_v[...], x_all[block(j)], preferred_element_type=F32)
        return moved.reshape(CB, CP, T).astype(BF)

    g_second = [gather_2(g_all, copy, k) for copy, k in zip(g_first[1:], ways)]
    for copy in [g_first[0]] + g_second:
        copy.wait_recv()
    load_down.wait()
    gh_v[...] = jnp.dot(down_v[...], g_all[...], preferred_element_type=F32)
    sq_sent.wait_recv()
    sq_ring[0] = sq_pair[0] + sq_pair[1]
    sq_parts = [send(sq_ring.at[0], sq_ring.at[k], at_y(k)) for k in range(1, RING)]

    x_second = []
    for at, k in ((2, 1), (3, 3), (1, 2)):
        x_second.append(gather_2(x_all, x_first[at], k))
    load_up.wait()
    for copy in [x_first[0]] + x_second:
        copy.wait_recv()
    xq_sent = {}
    for way in ways:
        px[way] = quarter((x + way) % RING * 2 + c)
        xq_sent[way] = send(px.at[way], xq.at[x, mine], at_x(way))

    for copy in sq_parts:
        copy.wait_recv()
    total = sq_ring[0] + sq_ring[1] + sq_ring[2] + sq_ring[3]
    radius = lax.rsqrt(total[:1] / D + norm_eps)

    def through(buf, lo, hi):
        raw = jnp.dot(up_v[lo:hi], x_all[...], preferred_element_type=F32)
        pre = radius * raw
        cdf = 0.5 * (1.0 + lax.erf(pre * half_root))
        slope = cdf + pre * jnp.exp(-0.5 * pre * pre) * pdf_scale
        hid_v[lo:hi] = (pre * cdf).astype(BF)
        back = radius * (gh_v[lo:hi] * slope)
        short = back.astype(BF)
        buf[x] = short
        gpr_v[lo:hi] = short
        sent = [send(buf.at[x], buf.at[x], at_x(k)) for k in (2, 1, 3)]
        return sent, jnp.sum(back * raw, axis=0, keepdims=True)

    gp_sent = []
    dots = jnp.zeros((1, T), F32)
    for buf, lo, hi in ((gp0, 0, FP), (gp1, FP, 2 * FP), (gp2, 2 * FP, F)):
        sent, dot = through(buf, lo, hi)
        gp_sent.append(sent)
        dots = dots + dot
    dots = jnp.broadcast_to(dots / D, (16, T))
    xq[x, mine] = quarter(x * 2 + c)
    xq[x, theirs] = quarter(x * 2 + other)

    out_t[...] = first_dims(down_v[...], hid_v[...])

    def block_of(k, core):
        return (y + k + RING) % RING * 2 + core

    def out_term(k, core):
        return out_t[block(block_of(k, core))]

    def grad_term(k, core):
        return grad_t[block(block_of(k, core))]

    pair_o, pair_g = {}, {}
    for at, k in enumerate((2, 1, 3, 0)):
        ps_o[at] = out_term(k, other).astype(BF)
        pair_o[k] = (at, send(ps_o.at[at], pr_o.at[at], partner))

    xq_shared = []
    for way in (1, 3, 2):
        source = (x - way + RING) % RING
        xq_sent[way].wait_recv()
        xq_shared.append(send(xq.at[source, mine], xq.at[source, mine], partner))

    grad_t[...] = first_dims(up_v[...], gpr_v[...])
    for at, k in enumerate((2, 1, 3, 0)):
        ps_g[at, :W] = grad_term(k, other).astype(BF)
        ps_g[at, W:] = dots.astype(BF)
        pair_g[k] = (at, send(ps_g.at[at], pr_g.at[at], partner))

    def out_sum(k):
        at, copy = pair_o[k]
        term = out_term(k, c)
        copy.wait_recv()
        return term + pr_o[at].astype(F32)

    def grad_sum(k):
        at, copy = pair_g[k]
        term = grad_term(k, c)
        copy.wait_recv()
        both = pr_g[at].astype(F32)
        return term + both[:W], dots + both[W:]

    for copy in xq_shared:
        copy.wait_recv()

    def left_rows(k):
        at = (z + k + NZ) % NZ
        return jnp.concatenate([xq[r, at] for r in range(RING)], axis=1)

    def turned(buf, lo, hi):
        return jnp.concatenate([buf[r, lo:hi] for r in range(RING)], axis=1)

    def term_of(buf):
        return lambda k: last_dims(left_rows(k), turned(buf, 0, FP))

    per = 128 // FL
    high = round_up(-(-CP // per), 16)
    lane_group = grid_of((high, 128), 1) // FL

    def rest_term(k):
        rest = turned(gp2, FP, FP + FL)
        wide_rest = last_dims(left_rows(k), jnp.concatenate([rest] * per, axis=0))
        folded = jnp.zeros((high, 128), F32)
        for g in range(per):
            rows = wide_rest[g * high : (g + 1) * high]
            if rows.shape[0] < high:
                pad = jnp.zeros((high - rows.shape[0], 128), F32)
                rows = jnp.concatenate([rows, pad], axis=0)
            folded = jnp.where(lane_group == g, rows, folded)
        return folded

    half = NZ // 2
    plan = (
        (term_of(gp0), zs0, zr0, 1),
        (term_of(gp1), zs1, zr1, -1),
        (term_of(gp2), zs2, zr2, 1),
        (rest_term, zs3, zr3, -1),
    )
    rings = []
    for term, sbuf, rbuf, way in plan:
        rings.append(((term, sbuf, rbuf, way, half, 0), []))
        rings.append(((term, sbuf, rbuf, -way, half - 1, half), []))

    def ring_step(ring, step):
        (term, sbuf, rbuf, way, length, base), sent = ring
        if step >= length:
            return
        at = base + step
        value = term(way * (length - step))
        if step > 0:
            sent[-1].wait_recv()
            value = value + rbuf[at - 1].astype(F32)
        sbuf[at] = value.astype(BF)
        sent.append(send(sbuf.at[at], rbuf.at[at], at_z(way)))

    def both_ways(piece, step):
        ring_step(rings[2 * piece], step)
        ring_step(rings[2 * piece + 1], step)

    for copy in gp_sent[0]:
        copy.wait_recv()
    both_ways(0, 0)
    o_sent = []
    for at, k in enumerate(ways):
        sb_o[at] = out_sum(k).astype(BF)
        o_sent.append(send(sb_o.at[at], rb_o.at[at], at_y(k)))
    for copy in gp_sent[1]:
        copy.wait_recv()
    both_ways(1, 0)
    g_sent = []
    for at, k in enumerate(ways):
        main, tail = grad_sum(k)
        sb_g[at, :W] = main.astype(BF)
        sb_g[at, W:] = tail.astype(BF)
        g_sent.append(send(sb_g.at[at], rb_g.at[at], at_y(k)))
    both_ways(0, 1)
    for copy in gp_sent[2]:
        copy.wait_recv()
    both_ways(2, 0)
    both_ways(3, 0)
    both_ways(1, 1)

    main = out_sum(0)
    for at, copy in enumerate(o_sent):
        copy.wait_recv()
        main = main + rb_o[at].astype(F32)
    tall[...] = jnp.zeros_like(tall)
    tall[:W] = main
    branch = jnp.transpose(tall[...])[:, :W]
    emb_v[...] = jnp.where(filled, placed_v[...] + scale_here * branch, 0.0).astype(BF)
    store_emb = pltpu.make_async_copy(emb_v, emb_out, osem.at[0])
    store_emb.start()

    both_ways(0, 2)
    both_ways(2, 1)
    both_ways(3, 1)
    both_ways(1, 2)

    main, tail = grad_sum(0)
    for at, copy in enumerate(g_sent):
        copy.wait_recv()
        main = main + rb_g[at, :W].astype(F32)
        tail = tail + rb_g[at, W:].astype(F32)
    tall[:W] = main
    tall[W:XW] = tail * (radius * radius)
    upright = jnp.transpose(tall[...])
    mean_dot = upright[:, W : W + 1]
    grad_in = gain_here * upright[:, :W] - placed_v[...] * mean_dot
    tg_v[...] = jnp.where(filled, gm_v[...] + grad_in, 0.0).astype(BF)
    store_tg = pltpu.make_async_copy(tg_v, tg_out, osem.at[1])
    store_tg.start()

    both_ways(0, 3)
    both_ways(2, 2)
    both_ways(3, 2)
    both_ways(1, 3)

    def ring_end(piece):
        value = rings[2 * piece][0][0](0)
        for (_, _, rbuf, _, length, base), sent in rings[2 * piece : 2 * piece + 2]:
            sent[-1].wait_recv()
            value = value + rbuf[base + length - 1].astype(F32)
        return value

    wg_v[:, :FP] = ring_end(0)[:CH].astype(BF)
    both_ways(2, 3)
    both_ways(3, 3)
    wg_v[:, FP : 2 * FP] = ring_end(1)[:CH].astype(BF)
    wg_v[:, 2 * FP : 3 * FP] = ring_end(2)[:CH].astype(BF)
    folded = ring_end(3)
    unfolded = [folded[:, g * FL : (g + 1) * FL] for g in range(per)]
    wg_v[:, 3 * FP :] = jnp.concatenate(unfolded, axis=0)[:CH].astype(BF)
    store_wg = pltpu.make_async_copy(wg_v, wg_out, osem.at[2])
    store_wg.start()

    for copy in used:
        copy.wait_send()
    store_emb.wait()
    store_tg.wait()
    store_wg.wait()
    assert len(used) <= n_copies, len(used)


def hand_over_kernel(a, b, c, a_out, b_out, c_out, a_v, b_v, c_v, sem):
    arrays = ((a, a_v, a_out), (b, b_v, b_out), (c, c_v, c_out))
    loads = [pltpu.make_async_copy(src, mid, sem.at[i]) for i, (src, mid, _) in enumerate(arrays)]
    stores = [pltpu.make_async_copy(mid, dst, sem.at[3 + i]) for i, (_, mid, dst) in enumerate(arrays)]
    for load in loads:
        load.start()
    for load, store in zip(loads, stores):
        load.wait()
        store.start()
    for store in stores:
        store.wait()


def hand_over(*arrays):
    hbm = pl.BlockSpec(memory_space=pl.ANY)
    return pl.pallas_call(
        hand_over_kernel,
        out_shape=tuple(jax.ShapeDtypeStruct(a.shape, a.dtype) for a in arrays),
        in_specs=[hbm] * 3,
        out_specs=(hbm,) * 3,
        scratch_shapes=[pltpu.VMEM(a.shape, a.dtype) for a in arrays]
        + [pltpu.SemaphoreType.DMA((6,))],
    )(*arrays)


def local(
    tiles, tile_counts, encoder_rank, out_grad, norm_gain, layer_scale, up_weight, down_weight
):
    slots, rows, width = tiles.shape
    ff = up_weight.shape[1]
    s = make_sizes(lax.axis_size("dp"), width, ff, slots, rows)
    NZ, W, F, T, DP = (s[k] for k in ("NZ", "W", "F", "T", "DP"))
    FP, FL, CB, CH, CP, XW, LW = (s[k] for k in ("FP", "FL", "CB", "CH", "CP", "XW", "LW"))
    D = W * 2 * RING
    n_copies = 160
    folded = (round_up(-(-CP // (128 // FL)), 16), 128)
    vm = pl.BlockSpec(memory_space=pltpu.VMEM)
    sm = pl.BlockSpec(memory_space=pltpu.SMEM)
    hbm = pl.BlockSpec(memory_space=pl.ANY)
    scratch = [
        pltpu.VMEM((F, D), BF),
        pltpu.VMEM((F, D), BF),
        pltpu.VMEM((T, W), BF),
        pltpu.VMEM((T, W), BF),
        pltpu.VMEM((T, W), BF),
        pltpu.VMEM((T, W), BF),
        pltpu.VMEM((CH, F), BF),
        pltpu.VMEM((DP, rows, W), BF),
        pltpu.VMEM((DP, rows, W), BF),
        pltpu.VMEM((D, T), BF),
        pltpu.VMEM((D, T), BF),
        pltpu.VMEM((2, 8, T), F32),
        pltpu.VMEM((RING, 8, T), F32),
        pltpu.VMEM((T, LW), F32),
        pltpu.VMEM((LW, T), F32),
        pltpu.VMEM((T, W), F32),
        pltpu.VMEM((T, W), F32),
        pltpu.VMEM((F, T), BF),
        pltpu.VMEM((F, T), BF),
        pltpu.VMEM((F, T), F32),
        pltpu.VMEM((D, T), F32),
        pltpu.VMEM((D, T), F32),
        pltpu.VMEM((CB * CP, W), BF),
        pltpu.VMEM((RING, CB, CP, T), BF),
        pltpu.VMEM((RING, 2 * CB, CP, T), BF),
        pltpu.VMEM((RING, FP, T), BF),
        pltpu.VMEM((RING, FP, T), BF),
        pltpu.VMEM((RING, FP + FL, T), BF),
        pltpu.VMEM((4, W, T), BF),
        pltpu.VMEM((4, W, T), BF),
        pltpu.VMEM((3, W, T), BF),
        pltpu.VMEM((3, W, T), BF),
        pltpu.VMEM((4, XW, T), BF),
        pltpu.VMEM((4, XW, T), BF),
        pltpu.VMEM((3, XW, T), BF),
        pltpu.VMEM((3, XW, T), BF),
    ]
    for _ in range(6):
        scratch.append(pltpu.VMEM((NZ, CP, FP), BF))
    for _ in range(2):
        scratch.append(pltpu.VMEM((NZ,) + folded, BF))
    scratch += [
        pltpu.SemaphoreType.DMA((4,)),
        pltpu.SemaphoreType.DMA((3,)),
        pltpu.SemaphoreType.DMA((n_copies,)),
        pltpu.SemaphoreType.DMA((n_copies,)),
    ]
    emb, tg, wg = pl.pallas_call(
        functools.partial(kernel, s, n_copies),
        out_shape=(
            jax.ShapeDtypeStruct((T, W), BF),
            jax.ShapeDtypeStruct((T, W), BF),
            jax.ShapeDtypeStruct((CH, F), BF),
        ),
        in_specs=[sm, sm, hbm, hbm, vm, vm, hbm, hbm],
        out_specs=(hbm, hbm, hbm),
        scratch_shapes=scratch,
        compiler_params=pltpu.CompilerParams(
            collective_id=0, has_side_effects=True, vmem_limit_bytes=56 * 2**20
        ),
    )(
        encoder_rank,
        tile_counts,
        tiles.reshape(T, W),
        out_grad.reshape(T, W),
        norm_gain,
        layer_scale,
        up_weight.T,
        down_weight.T,
    )
    emb, tg, wg = hand_over(emb, tg, wg)
    return emb.reshape(tiles.shape), tg.reshape(tiles.shape), wg


def solution(mesh):
    in_specs = (
        P("dp", None, "mp"),
        P(),
        P(),
        P("dp", None, "mp"),
        P(),
        P(),
        P(None, "mp"),
        P(None, "mp"),
    )
    out_specs = (P("dp", None, "mp"), P("dp", None, "mp"), P("dp", "mp"))
    return jax.shard_map(local, mesh=mesh, in_specs=in_specs, out_specs=out_specs, check_vma=False)
```

time: 87.2 us -> 64.2 us (0.74)
  Pallas kernels: 86.3 us -> 63.3 us
    pallas_call x1, Pallas kernels: 14.7 us -> 1.78 us  [hand_over(): pl.pallas_call(hand_over_kernel, out_shape=tuple((jax.ShapeDtypeStruct(a....]
    pallas_call x1, Pallas kernels: 71.6 us -> 61.5 us  [local(): pl.pallas_call(functools.partial(kernel, s, n_copies), out_shape=(jax.Sha...]
where the time goes in v3:
time: 64.2 us; the launch traced here: 63.9 us
  Pallas kernels  63.3 us (99%)
    pallas_call x1, Pallas kernels, local(): pl.pallas_call(functools.partial(kernel, s, n_copies), out_shape=(jax.Sha...  61.5 us
    pallas_call x1, Pallas kernels, hand_over(): pl.pallas_call(hand_over_kernel, out_shape=tuple((jax.ShapeDtypeStruct(a....  1.78 us

profile of v3, /device:TPU:32, one launch (start us, length us, event | category | flops | bytes accessed | tf_op | source)
XLA Modules:
  0.0 63.9 jit_solution(6707840078259233067)
XLA Ops:
  0.6 61.5 %shard_map.103 = (bf16[128,400]{1,0:T(8,128)(2,1)}, bf16[128,400]{1,0:T(8,128)(2,1)}, bf16[100,800]{1,0:T(8,128)(2,1)}) custom-call(s32[512]{0:T(512)} %enc.1, s32[64]{0:T(128)} %cnt.1, bf16[128,400]{1,0:T(8,128)(2,1)} %bitcast.8, bf16[128,400]{1,0:T(8,128)(2,1)} %bitcast.9, f32[3200]{0:T(1024)} %gain.1, f32[3200]{0:T(1024)} %scale.1, ...), custom_call_target="tpu_custom_call" | custom-call | tf_op jit(solution)/shard_map/pallas_call | solution.py:543
  62.1 1.8 %shard_map.104 = (bf16[128,400]{1,0:T(8,128)(2,1)}, bf16[128,400]{1,0:T(8,128)(2,1)}, bf16[100,800]{1,0:T(8,128)(2,1)}) custom-call(bf16[128,400]{1,0:T(8,128)(2,1)} %get-tuple-element.9.a, bf16[128,400]{1,0:T(8,128)(2,1)} %get-tuple-element.10.b, bf16[100,800]{1,0:T(8,128)(2,1)} %get-tuple-element.11.c), custom_call_target="tpu_custom_call" | custom-call | tf_op jit(solution)/shard_map/pallas_call | solution.py:471

commit v4 on v3

--- a/solution.py
+++ b/solution.py
@@ -52,14 +52,14 @@
 
 def kernel(
     s, n_copies,
-    enc, cnt, tiles_hbm, grad_hbm, gain, scale, up_hbm, down_hbm,
+    enc_hbm, cnt_hbm, tiles_hbm, grad_hbm, gain_hbm, scale_hbm, up_hbm, down_hbm,
     emb_out, tg_out, wg_out,
-    up_v, down_v, tiles, out_grad, emb_v, tg_v, wg_v,
+    enc, cnt, gain, scale, up_v, down_v, tiles, out_grad, emb_v, tg_v, wg_v,
     out1, in1, g_all, x_all, sq_pair, sq_ring, wide, tall, placed_v, gm_v,
     hid_v, gpr_v, gh_v, out_t, grad_t, sel_v, px, xq, gp0, gp1, gp2,
     ps_o, pr_o, sb_o, rb_o, ps_g, pr_g, sb_g, rb_g,
     zs0, zr0, zs1, zr1, zs2, zr2, zs3, zr3,
-    wsem, osem, send_sem, recv_sem,
+    wsem, osem, sems,
 ):
     NZ, W, F, SLOTS, R, T, DP = (s[k] for k in ("NZ", "W", "F", "SLOTS", "R", "T", "DP"))
     FP, FL, CB, CH, CP, XW, LW = (s[k] for k in ("FP", "FL", "CB", "CH", "CP", "XW", "LW"))
@@ -83,17 +83,37 @@
         return {"dp": dp, "mp": (y + k + RING) % RING * 2 + c}
 
     partner = {"dp": dp, "mp": y * 2 + other}
-    used = []
-
-    def send(src, dst, device):
-        at = len(used)
+    taken = []
+    sent_later = []
+
+    def new():
+        taken.append(len(taken))
+        return taken[-1]
+
+    def send(src, dst, device, sent, got):
         copy = pltpu.make_async_remote_copy(
-            src_ref=src, dst_ref=dst, send_sem=send_sem.at[at], recv_sem=recv_sem.at[at],
+            src_ref=src, dst_ref=dst, send_sem=sems.at[sent], recv_sem=sems.at[got],
             device_id=device, device_id_type=pl.DeviceIdType.MESH,
         )
         copy.start()
-        used.append(copy)
-        return copy
+
+    def wait(at, like):
+        pltpu.make_async_copy(like, like, sems.at[at]).wait()
+
+    def outgoing(like):
+        at = new()
+        sent_later.append((at, like))
+        return at
+
+    smalls = []
+    for at, (src, dst) in enumerate(
+        ((enc_hbm, enc), (cnt_hbm, cnt), (gain_hbm, gain), (scale_hbm, scale))
+    ):
+        smalls.append(pltpu.make_async_copy(src, dst, wsem.at[4 + at]))
+    first = pltpu.make_async_copy(tiles_hbm, tiles, wsem.at[0])
+    second = pltpu.make_async_copy(grad_hbm, out_grad, wsem.at[1])
+    for small in smalls[:2] + [first] + smalls[2:] + [second]:
+        small.start()
 
     barrier = pltpu.get_barrier_semaphore()
     others = [(i, k) for k in range(NZ) for i in range(RING) if (i, k) != (0, 0)]
@@ -103,10 +123,6 @@
     for device in peers:
         pl.semaphore_signal(barrier, inc=1, device_id=device, device_id_type=pl.DeviceIdType.MESH)
 
-    first = pltpu.make_async_copy(tiles_hbm, tiles, wsem.at[0])
-    first.start()
-    second = pltpu.make_async_copy(grad_hbm, out_grad, wsem.at[1])
-    second.start()
     load_down = pltpu.make_async_copy(down_hbm, down_v, wsem.at[2])
     load_down.start()
     load_up = pltpu.make_async_copy(up_hbm, up_v, wsem.at[3])
@@ -119,6 +135,8 @@
         return pl.ds(pl.multiple_of(j * W + lo, 16), size)
 
     lane = grid_of((1, T), 1)
+    smalls[0].wait()
+    smalls[1].wait()
     dest = jnp.full((1, T), -1, jnp.int32)
     for j in range(SLOTS):
         live = (j % 8) < cnt[dp * (SLOTS // 8) + j // 8]
@@ -132,10 +150,10 @@
     out1[...] = picked.reshape(DP, R, W).astype(BF)
 
     pl.semaphore_wait(barrier, len(peers))
-    exchange = []
+    ex_out, ex_in = outgoing(out1.at[pl.ds(0, DP - 1)]), new()
     for i, k in others:
         there = (x + i) % RING * NZ + (z + k) % NZ
-        exchange.append(send(out1.at[there], in1.at[dp], at_xz(i, k)))
+        send(out1.at[there], in1.at[dp], at_xz(i, k), ex_out, ex_in)
     in1[dp] = out1[dp]
 
     lane_all = grid_of((1, rows_all), 1) // R
@@ -164,6 +182,8 @@
             part = jnp.where(mp == j, whole[:, j * W : (j + 1) * W], part)
         return part
 
+    smalls[2].wait()
+    smalls[3].wait()
     gain_here = local_part(gain)
     scale_here = local_part(scale)
 
@@ -176,16 +196,24 @@
 
     ways = (2, 1, 3)
 
-    def gather_1(buf):
+    seven = pl.ds(0, 7 * W)
+    four = pl.ds(0, 4 * W)
+    three = pl.ds(0, 3 * W)
+    one = pl.ds(0, W)
+    inner = pl.ds(1, RING - 1)
+
+    def gather_1(buf, sent, pair, along):
         own = buf.at[block(mp)]
-        return [send(own, own, partner)] + [send(own, own, at_y(k)) for k in ways]
-
-    def gather_2(buf, copy, k):
-        copy.wait_recv()
+        send(own, own, partner, sent, pair)
+        for k in ways:
+            send(own, own, at_y(k), sent, along[k])
+
+    def gather_2(buf, k, sent, pair):
         piece = buf.at[block((y - k + RING) % RING * 2 + c)]
-        return send(piece, piece, partner)
-
-    g_first = gather_1(g_all)
+        send(piece, piece, partner, sent, pair)
+
+    g_out, g_pair, g_along = outgoing(g_all.at[seven]), new(), new()
+    gather_1(g_all, g_out, g_pair, {k: g_along for k in ways})
 
     pack_row = grid_of((T, rows_all), 0)
     packer = ((pack_row // R) == order) & (
@@ -202,19 +230,24 @@
             & (sel_row < k * CP + CH)
         )
     sel_v[...] = sel.astype(BF)
-
-    for copy in exchange:
-        copy.wait_recv()
+    sel_row = grid_of((CP, W), 0)
+    sel_y = ((sel_row + y * CH) == grid_of((CP, W), 1)) & (sel_row < CH)
+    sel_y = sel_y.astype(BF)
+
+    wait(ex_in, in1.at[pl.ds(0, DP - 1)])
     arrived = in1[...].astype(F32).reshape(rows_all, W).astype(BF)
     placed = jnp.dot(packer, arrived, preferred_element_type=F32)
     placed_v[...] = placed
     wide[:, :W] = placed * gain_here
     x_all[block(mp)] = jnp.transpose(wide[...])[:W].astype(BF)
-    x_first = gather_1(x_all)
+    x_out, x_pair = outgoing(x_all.at[seven]), new()
+    x_along = {k: new() for k in ways}
+    gather_1(x_all, x_out, x_pair, x_along)
     wide[:, :W] = placed * placed
     squares = jnp.sum(jnp.transpose(wide[...]), axis=0, keepdims=True)
     sq_pair[0] = jnp.broadcast_to(squares, (8, T))
-    sq_sent = send(sq_pair.at[0], sq_pair.at[1], partner)
+    sq_got = new()
+    send(sq_pair.at[0], sq_pair.at[1], partner, outgoing(sq_pair.at[0]), sq_got)
 
     mine = pl.ds(c * CB, CB)
     theirs = pl.ds(other * CB, CB)
@@ -223,28 +256,30 @@
         moved = jnp.dot(sel_v[...], x_all[block(j)], preferred_element_type=F32)
         return moved.reshape(CB, CP, T).astype(BF)
 
-    g_second = [gather_2(g_all, copy, k) for copy, k in zip(g_first[1:], ways)]
-    for copy in [g_first[0]] + g_second:
-        copy.wait_recv()
+    wait(g_along, g_all.at[three])
+    for k in ways:
+        gather_2(g_all, k, g_out, g_pair)
+    wait(g_pair, g_all.at[four])
     load_down.wait()
     gh_v[...] = jnp.dot(down_v[...], g_all[...], preferred_element_type=F32)
-    sq_sent.wait_recv()
+    wait(sq_got, sq_pair.at[0])
     sq_ring[0] = sq_pair[0] + sq_pair[1]
-    sq_parts = [send(sq_ring.at[0], sq_ring.at[k], at_y(k)) for k in range(1, RING)]
-
-    x_second = []
-    for at, k in ((2, 1), (3, 3), (1, 2)):
-        x_second.append(gather_2(x_all, x_first[at], k))
+    sq_out, sq_in = outgoing(sq_ring.at[inner]), new()
+    for k in ways:
+        send(sq_ring.at[0], sq_ring.at[k], at_y(k), sq_out, sq_in)
+
+    for k in ways:
+        wait(x_along[k], x_all.at[one])
+        gather_2(x_all, k, x_out, x_pair)
     load_up.wait()
-    for copy in [x_first[0]] + x_second:
-        copy.wait_recv()
-    xq_sent = {}
+    wait(x_pair, x_all.at[four])
+    part_y = c * CB + y
+    xq_out, xq_in = outgoing(px), new()
     for way in ways:
-        px[way] = quarter((x + way) % RING * 2 + c)
-        xq_sent[way] = send(px.at[way], xq.at[x, mine], at_x(way))
-
-    for copy in sq_parts:
-        copy.wait_recv()
+        piece = x_all[block((x + way) % RING * 2 + c)]
+        px[way - 1] = jnp.dot(sel_y, piece, preferred_element_type=F32).astype(BF)
+        send(px.at[way - 1], xq.at[way, part_y], at_x(way), xq_out, xq_in)
+    wait(sq_in, sq_ring.at[inner])
     total = sq_ring[0] + sq_ring[1] + sq_ring[2] + sq_ring[3]
     radius = lax.rsqrt(total[:1] / D + norm_eps)
 
@@ -256,20 +291,27 @@
         hid_v[lo:hi] = (pre * cdf).astype(BF)
         back = radius * (gh_v[lo:hi] * slope)
         short = back.astype(BF)
-        buf[x] = short
+        buf[0] = short
         gpr_v[lo:hi] = short
-        sent = [send(buf.at[x], buf.at[x], at_x(k)) for k in (2, 1, 3)]
-        return sent, jnp.sum(back * raw, axis=0, keepdims=True)
-
-    gp_sent = []
+        sent, got = outgoing(buf.at[inner]), new()
+        for k in ways:
+            send(buf.at[0], buf.at[k], at_x(k), sent, got)
+        return got, jnp.sum(back * raw, axis=0, keepdims=True)
+
+    gp_in = []
     dots = jnp.zeros((1, T), F32)
-    for buf, lo, hi in ((gp0, 0, FP), (gp1, FP, 2 * FP), (gp2, 2 * FP, F)):
-        sent, dot = through(buf, lo, hi)
-        gp_sent.append(sent)
+    for buf, lo, hi in ((gp0, 0, FP + FL), (gp1, FP + FL, 2 * FP + FL), (gp2, 2 * FP + FL, F)):
+        got, dot = through(buf, lo, hi)
+        gp_in.append(got)
         dots = dots + dot
     dots = jnp.broadcast_to(dots / D, (16, T))
-    xq[x, mine] = quarter(x * 2 + c)
-    xq[x, theirs] = quarter(x * 2 + other)
+    wait(xq_in, px)
+    xq_y_out, xq_y_in = outgoing(xq.at[inner, inner]), new()
+    for k in ways:
+        piece = xq.at[inner, part_y]
+        send(piece, piece, at_y(k), xq_y_out, xq_y_in)
+    xq[0, mine] = quarter(x * 2 + c)
+    xq[0, theirs] = quarter(x * 2 + other)
 
     out_t[...] = first_dims(down_v[...], hid_v[...])
 
@@ -282,38 +324,37 @@
     def grad_term(k, core):
         return grad_t[block(block_of(k, core))]
 
-    pair_o, pair_g = {}, {}
-    for at, k in enumerate((2, 1, 3, 0)):
+    order = (2, 1, 3, 0)
+    po_out, po_in = outgoing(ps_o), new()
+    for at, k in enumerate(order):
         ps_o[at] = out_term(k, other).astype(BF)
-        pair_o[k] = (at, send(ps_o.at[at], pr_o.at[at], partner))
-
-    xq_shared = []
-    for way in (1, 3, 2):
-        source = (x - way + RING) % RING
-        xq_sent[way].wait_recv()
-        xq_shared.append(send(xq.at[source, mine], xq.at[source, mine], partner))
+        send(ps_o.at[at], pr_o.at[at], partner, po_out, po_in)
 
     grad_t[...] = first_dims(up_v[...], gpr_v[...])
-    for at, k in enumerate((2, 1, 3, 0)):
+    pg_out, pg_in = outgoing(ps_g), new()
+    for at, k in enumerate(order):
         ps_g[at, :W] = grad_term(k, other).astype(BF)
         ps_g[at, W:] = dots.astype(BF)
-        pair_g[k] = (at, send(ps_g.at[at], pr_g.at[at], partner))
-
-    def out_sum(k):
-        at, copy = pair_o[k]
-        term = out_term(k, c)
-        copy.wait_recv()
-        return term + pr_o[at].astype(F32)
-
-    def grad_sum(k):
-        at, copy = pair_g[k]
-        term = grad_term(k, c)
-        copy.wait_recv()
+        send(ps_g.at[at], pr_g.at[at], partner, pg_out, pg_in)
+
+    def out_sum(at):
+        return out_term(order[at], c) + pr_o[at].astype(F32)
+
+    def grad_sum(at):
         both = pr_g[at].astype(F32)
-        return term + both[:W], dots + both[W:]
-
-    for copy in xq_shared:
-        copy.wait_recv()
+        return grad_term(order[at], c) + both[:W], dots + both[W:]
+
+    wait(po_in, pr_o)
+    so_out, so_in = outgoing(sb_o), new()
+    for at, k in enumerate(ways):
+        sb_o[at] = out_sum(at).astype(BF)
+        send(sb_o.at[at], rb_o.at[at], at_y(k), so_out, so_in)
+
+    wait(xq_y_in, xq.at[inner, inner])
+    xq_p_in = new()
+    piece = xq.at[inner, mine]
+    send(piece, piece, partner, outgoing(piece), xq_p_in)
+    wait(xq_p_in, xq.at[inner, theirs])
 
     def left_rows(k):
         at = (z + k + NZ) % NZ
@@ -330,7 +371,7 @@
     lane_group = grid_of((high, 128), 1) // FL
 
     def rest_term(k):
-        rest = turned(gp2, FP, FP + FL)
+        rest = turned(gp0, FP, FP + FL)
         wide_rest = last_dims(left_rows(k), jnp.concatenate([rest] * per, axis=0))
         folded = jnp.zeros((high, 128), F32)
         for g in range(per):
@@ -350,51 +391,48 @@
     )
     rings = []
     for term, sbuf, rbuf, way in plan:
-        rings.append(((term, sbuf, rbuf, way, half, 0), []))
-        rings.append(((term, sbuf, rbuf, -way, half - 1, half), []))
+        z_out = outgoing(sbuf.at[pl.ds(0, NZ - 1)])
+        rings.append(((term, sbuf, rbuf, way, half, 0), z_out, []))
+        rings.append(((term, sbuf, rbuf, -way, half - 1, half), z_out, []))
 
     def ring_step(ring, step):
-        (term, sbuf, rbuf, way, length, base), sent = ring
+        (term, sbuf, rbuf, way, length, base), z_out, got = ring
         if step >= length:
             return
         at = base + step
         value = term(way * (length - step))
         if step > 0:
-            sent[-1].wait_recv()
+            wait(got[-1], rbuf.at[at - 1])
             value = value + rbuf[at - 1].astype(F32)
         sbuf[at] = value.astype(BF)
-        sent.append(send(sbuf.at[at], rbuf.at[at], at_z(way)))
+        got.append(new())
+        send(sbuf.at[at], rbuf.at[at], at_z(way), z_out, got[-1])
 
     def both_ways(piece, step):
         ring_step(rings[2 * piece], step)
         ring_step(rings[2 * piece + 1], step)
 
-    for copy in gp_sent[0]:
-        copy.wait_recv()
+    wait(gp_in[0], gp0.at[inner])
     both_ways(0, 0)
-    o_sent = []
+    both_ways(3, 0)
+    wait(gp_in[1], gp1.at[inner])
+    both_ways(1, 0)
+    wait(pg_in, pr_g)
+    sg_out, sg_in = outgoing(sb_g), new()
     for at, k in enumerate(ways):
-        sb_o[at] = out_sum(k).astype(BF)
-        o_sent.append(send(sb_o.at[at], rb_o.at[at], at_y(k)))
-    for copy in gp_sent[1]:
-        copy.wait_recv()
-    both_ways(1, 0)
-    g_sent = []
-    for at, k in enumerate(ways):
-        main, tail = grad_sum(k)
+        main, tail = grad_sum(at)
         sb_g[at, :W] = main.astype(BF)
         sb_g[at, W:] = tail.astype(BF)
-        g_sent.append(send(sb_g.at[at], rb_g.at[at], at_y(k)))
+        send(sb_g.at[at], rb_g.at[at], at_y(k), sg_out, sg_in)
     both_ways(0, 1)
-    for copy in gp_sent[2]:
-        copy.wait_recv()
+    both_ways(3, 1)
+    wait(gp_in[2], gp2.at[inner])
     both_ways(2, 0)
-    both_ways(3, 0)
     both_ways(1, 1)
 
-    main = out_sum(0)
-    for at, copy in enumerate(o_sent):
-        copy.wait_recv()
+    main = out_sum(3)
+    wait(so_in, rb_o)
+    for at in range(RING - 1):
         main = main + rb_o[at].astype(F32)
     tall[...] = jnp.zeros_like(tall)
     tall[:W] = main
@@ -404,13 +442,13 @@
     store_emb.start()
 
     both_ways(0, 2)
+    both_ways(3, 2)
     both_ways(2, 1)
-    both_ways(3, 1)
     both_ways(1, 2)
 
-    main, tail = grad_sum(0)
-    for at, copy in enumerate(g_sent):
-        copy.wait_recv()
+    main, tail = grad_sum(3)
+    wait(sg_in, rb_g)
+    for at in range(RING - 1):
         main = main + rb_g[at, :W].astype(F32)
         tail = tail + rb_g[at, W:].astype(F32)
     tall[:W] = main
@@ -423,34 +461,34 @@
     store_tg.start()
 
     both_ways(0, 3)
+    both_ways(3, 3)
     both_ways(2, 2)
-    both_ways(3, 2)
     both_ways(1, 3)
 
     def ring_end(piece):
         value = rings[2 * piece][0][0](0)
-        for (_, _, rbuf, _, length, base), sent in rings[2 * piece : 2 * piece + 2]:
-            sent[-1].wait_recv()
+        for (_, _, rbuf, _, length, base), _, got in rings[2 * piece : 2 * piece + 2]:
+            wait(got[-1], rbuf.at[base + length - 1])
             value = value + rbuf[base + length - 1].astype(F32)
         return value
 
     wg_v[:, :FP] = ring_end(0)[:CH].astype(BF)
     both_ways(2, 3)
-    both_ways(3, 3)
-    wg_v[:, FP : 2 * FP] = ring_end(1)[:CH].astype(BF)
-    wg_v[:, 2 * FP : 3 * FP] = ring_end(2)[:CH].astype(BF)
     folded = ring_end(3)
     unfolded = [folded[:, g * FL : (g + 1) * FL] for g in range(per)]
-    wg_v[:, 3 * FP :] = jnp.concatenate(unfolded, axis=0)[:CH].astype(BF)
+    rest = jnp.concatenate(unfolded, axis=0)[:CH]
+    wg_v[:, FP : FP + FL] = rest.astype(BF)
+    wg_v[:, FP + FL : 2 * FP + FL] = ring_end(1)[:CH].astype(BF)
+    wg_v[:, 2 * FP + FL :] = ring_end(2)[:CH].astype(BF)
     store_wg = pltpu.make_async_copy(wg_v, wg_out, osem.at[2])
     store_wg.start()
 
-    for copy in used:
-        copy.wait_send()
+    for at, like in sent_later:
+        wait(at, like)
     store_emb.wait()
     store_tg.wait()
     store_wg.wait()
-    assert len(used) <= n_copies, len(used)
+    assert len(taken) == n_copies, len(taken)
 
 
 def hand_over_kernel(a, b, c, a_out, b_out, c_out, a_v, b_v, c_v, sem):
@@ -487,12 +525,14 @@
     NZ, W, F, T, DP = (s[k] for k in ("NZ", "W", "F", "T", "DP"))
     FP, FL, CB, CH, CP, XW, LW = (s[k] for k in ("FP", "FL", "CB", "CH", "CP", "XW", "LW"))
     D = W * 2 * RING
-    n_copies = 160
+    n_copies = 66
     folded = (round_up(-(-CP // (128 // FL)), 16), 128)
-    vm = pl.BlockSpec(memory_space=pltpu.VMEM)
-    sm = pl.BlockSpec(memory_space=pltpu.SMEM)
     hbm = pl.BlockSpec(memory_space=pl.ANY)
     scratch = [
+        pltpu.SMEM((DP * slots,), jnp.int32),
+        pltpu.SMEM((DP * slots // 8,), jnp.int32),
+        pltpu.VMEM((D,), F32),
+        pltpu.VMEM((D,), F32),
         pltpu.VMEM((F, D), BF),
         pltpu.VMEM((F, D), BF),
         pltpu.VMEM((T, W), BF),
@@ -516,11 +556,11 @@
         pltpu.VMEM((D, T), F32),
         pltpu.VMEM((D, T), F32),
         pltpu.VMEM((CB * CP, W), BF),
-        pltpu.VMEM((RING, CB, CP, T), BF),
+        pltpu.VMEM((RING - 1, CP, T), BF),
         pltpu.VMEM((RING, 2 * CB, CP, T), BF),
+        pltpu.VMEM((RING, FP + FL, T), BF),
         pltpu.VMEM((RING, FP, T), BF),
         pltpu.VMEM((RING, FP, T), BF),
-        pltpu.VMEM((RING, FP + FL, T), BF),
         pltpu.VMEM((4, W, T), BF),
         pltpu.VMEM((4, W, T), BF),
         pltpu.VMEM((3, W, T), BF),
@@ -535,9 +575,8 @@
     for _ in range(2):
         scratch.append(pltpu.VMEM((NZ,) + folded, BF))
     scratch += [
-        pltpu.SemaphoreType.DMA((4,)),
+        pltpu.SemaphoreType.DMA((8,)),
         pltpu.SemaphoreType.DMA((3,)),
-        pltpu.SemaphoreType.DMA((n_copies,)),
         pltpu.SemaphoreType.DMA((n_copies,)),
     ]
     emb, tg, wg = pl.pallas_call(
@@ -547,7 +586,7 @@
             jax.ShapeDtypeStruct((T, W), BF),
             jax.ShapeDtypeStruct((CH, F), BF),
         ),
-        in_specs=[sm, sm, hbm, hbm, vm, vm, hbm, hbm],
+        in_specs=[hbm] * 8,
         out_specs=(hbm, hbm, hbm),
         scratch_shapes=scratch,
         compiler_params=pltpu.CompilerParams(

time: 64.2 us -> 63 us (0.981)
  Pallas kernels: 63.3 us -> 62.3 us
    pallas_call x1, Pallas kernels: 61.5 us -> 60.5 us  [local(): pl.pallas_call(functools.partial(kernel, s, n_copies), out_shape=(jax.Sha...]
where the time goes in v4:
time: 63 us; the launch traced here: 62.9 us
  Pallas kernels  62.3 us (99%)
  between operations  0.64 us (1%)
    pallas_call x1, Pallas kernels, local(): pl.pallas_call(functools.partial(kernel, s, n_copies), out_shape=(jax.Sha...  60.5 us
    pallas_call x1, Pallas kernels, hand_over(): pl.pallas_call(hand_over_kernel, out_shape=tuple((jax.ShapeDtypeStruct(a....  1.78 us

profile of v4, /device:TPU:32, one launch (start us, length us, event | category | flops | bytes accessed | tf_op | source)
XLA Modules:
  0.0 62.9 jit_solution(3744253839473844485)
XLA Ops:
  0.6 60.5 %shard_map.103 = (bf16[128,400]{1,0:T(8,128)(2,1)}, bf16[128,400]{1,0:T(8,128)(2,1)}, bf16[100,800]{1,0:T(8,128)(2,1)}) custom-call(s32[512]{0:T(512)} %enc_hbm.1, s32[64]{0:T(128)} %cnt_hbm.1, bf16[128,400]{1,0:T(8,128)(2,1)} %bitcast.8, bf16[128,400]{1,0:T(8,128)(2,1)} %bitcast.9, f32[3200]{0:T(1024)} %gain_hbm.1, f32[3200]{0:T(1024)} %scale_hbm.1, ...), custom_call_target="tpu_custom_call" | custom-call | tf_op jit(solution)/shard_map/pallas_call | solution.py:582
  61.1 1.8 %shard_map.104 = (bf16[128,400]{1,0:T(8,128)(2,1)}, bf16[128,400]{1,0:T(8,128)(2,1)}, bf16[100,800]{1,0:T(8,128)(2,1)}) custom-call(bf16[128,400]{1,0:T(8,128)(2,1)} %get-tuple-element.9.a, bf16[128,400]{1,0:T(8,128)(2,1)} %get-tuple-element.10.b, bf16[100,800]{1,0:T(8,128)(2,1)} %get-tuple-element.11.c), custom_call_target="tpu_custom_call" | custom-call | tf_op jit(solution)/shard_map/pallas_call | solution.py:509

commit v5 on v4

--- a/solution.py
+++ b/solution.py
@@ -56,9 +56,9 @@
     emb_out, tg_out, wg_out,
     enc, cnt, gain, scale, up_v, down_v, tiles, out_grad, emb_v, tg_v, wg_v,
     out1, in1, g_all, x_all, sq_pair, sq_ring, wide, tall, placed_v, gm_v,
-    hid_v, gpr_v, gh_v, out_t, grad_t, sel_v, px, xq, gp0, gp1, gp2,
+    hid_v, gpr_v, gh_v, acc_v, out_t, grad_t, sel_v, px, xq, gp0, gp1, gp2,
     ps_o, pr_o, sb_o, rb_o, ps_g, pr_g, sb_g, rb_g,
-    zs0, zr0, zs1, zr1, zs2, zr2, zs3, zr3,
+    xl_v, zt0, zt1, zt2, zt3, zs0, zr0, zs1, zr1, zs2, zr2, zs3, zr3,
     wsem, osem, sems,
 ):
     NZ, W, F, SLOTS, R, T, DP = (s[k] for k in ("NZ", "W", "F", "SLOTS", "R", "T", "DP"))
@@ -271,20 +271,27 @@
     for k in ways:
         wait(x_along[k], x_all.at[one])
         gather_2(x_all, k, x_out, x_pair)
+    for parity in range(2):
+
+        @pl.when(c == parity)
+        def _():
+            for at in range(RING):
+                lo = (2 * at + parity) * W
+                moved = jnp.dot(sel_y, x_all[lo : lo + W], preferred_element_type=F32)
+                px[at] = moved.astype(BF)
+
+    part_y = c * CB + y
+    xq_out, xq_in = outgoing(px.at[pl.ds(0, RING - 1)]), new()
+    for way in ways:
+        send(px.at[(x + way) % RING], xq.at[way, part_y], at_x(way), xq_out, xq_in)
     load_up.wait()
     wait(x_pair, x_all.at[four])
-    part_y = c * CB + y
-    xq_out, xq_in = outgoing(px), new()
-    for way in ways:
-        piece = x_all[block((x + way) % RING * 2 + c)]
-        px[way - 1] = jnp.dot(sel_y, piece, preferred_element_type=F32).astype(BF)
-        send(px.at[way - 1], xq.at[way, part_y], at_x(way), xq_out, xq_in)
     wait(sq_in, sq_ring.at[inner])
     total = sq_ring[0] + sq_ring[1] + sq_ring[2] + sq_ring[3]
     radius = lax.rsqrt(total[:1] / D + norm_eps)
 
     def through(buf, lo, hi):
-        raw = jnp.dot(up_v[lo:hi], x_all[...], preferred_element_type=F32)
+        raw = acc_v[lo:hi]
         pre = radius * raw
         cdf = 0.5 * (1.0 + lax.erf(pre * half_root))
         slope = cdf + pre * jnp.exp(-0.5 * pre * pre) * pdf_scale
@@ -298,6 +305,7 @@
             send(buf.at[0], buf.at[k], at_x(k), sent, got)
         return got, jnp.sum(back * raw, axis=0, keepdims=True)
 
+    acc_v[...] = jnp.dot(up_v[...], x_all[...], preferred_element_type=F32)
     gp_in = []
     dots = jnp.zeros((1, T), F32)
     for buf, lo, hi in ((gp0, 0, FP + FL), (gp1, FP + FL, 2 * FP + FL), (gp2, 2 * FP + FL, F)):
@@ -305,11 +313,14 @@
         gp_in.append(got)
         dots = dots + dot
     dots = jnp.broadcast_to(dots / D, (16, T))
-    wait(xq_in, px)
-    xq_y_out, xq_y_in = outgoing(xq.at[inner, inner]), new()
+    wait(xq_in, px.at[pl.ds(0, RING - 1)])
+    share_out, share_in = outgoing(xq.at[inner, mine]), new()
+    piece = xq.at[inner, part_y]
+    send(piece, piece, partner, share_out, share_in)
+    xq_y_out = outgoing(xq.at[inner, inner])
+    xq_y_in = {k: new() for k in ways}
     for k in ways:
-        piece = xq.at[inner, part_y]
-        send(piece, piece, at_y(k), xq_y_out, xq_y_in)
+        send(piece, piece, at_y(k), xq_y_out, xq_y_in[k])
     xq[0, mine] = quarter(x * 2 + c)
     xq[0, theirs] = quarter(x * 2 + other)
 
@@ -350,29 +361,30 @@
         sb_o[at] = out_sum(at).astype(BF)
         send(sb_o.at[at], rb_o.at[at], at_y(k), so_out, so_in)
 
-    wait(xq_y_in, xq.at[inner, inner])
-    xq_p_in = new()
-    piece = xq.at[inner, mine]
-    send(piece, piece, partner, outgoing(piece), xq_p_in)
-    wait(xq_p_in, xq.at[inner, theirs])
-
-    def left_rows(k):
-        at = (z + k + NZ) % NZ
-        return jnp.concatenate([xq[r, at] for r in range(RING)], axis=1)
+    for k in (1, 3, 2):
+        piece = xq.at[inner, c * CB + (y - k + RING) % RING]
+        wait(xq_y_in[k], piece)
+        send(piece, piece, partner, share_out, share_in)
+    wait(share_in, xq.at[inner, theirs])
+
+    for k in range(NZ):
+        xl_v[k * CP : (k + 1) * CP] = jnp.concatenate([xq[r, k] for r in range(RING)], axis=1)
 
     def turned(buf, lo, hi):
         return jnp.concatenate([buf[r, lo:hi] for r in range(RING)], axis=1)
 
-    def term_of(buf):
-        return lambda k: last_dims(left_rows(k), turned(buf, 0, FP))
+    def terms(right, into):
+        into[...] = last_dims(xl_v[...], right).reshape(NZ, CP, right.shape[0])
+
+    def term_of(into):
+        return lambda k: into[(z + k + NZ) % NZ]
 
     per = 128 // FL
     high = round_up(-(-CP // per), 16)
     lane_group = grid_of((high, 128), 1) // FL
 
     def rest_term(k):
-        rest = turned(gp0, FP, FP + FL)
-        wide_rest = last_dims(left_rows(k), jnp.concatenate([rest] * per, axis=0))
+        wide_rest = zt3[(z + k + NZ) % NZ]
         folded = jnp.zeros((high, 128), F32)
         for g in range(per):
             rows = wide_rest[g * high : (g + 1) * high]
@@ -384,9 +396,9 @@
 
     half = NZ // 2
     plan = (
-        (term_of(gp0), zs0, zr0, 1),
-        (term_of(gp1), zs1, zr1, -1),
-        (term_of(gp2), zs2, zr2, 1),
+        (term_of(zt0), zs0, zr0, 1),
+        (term_of(zt1), zs1, zr1, -1),
+        (term_of(zt2), zs2, zr2, 1),
         (rest_term, zs3, zr3, -1),
     )
     rings = []
@@ -413,9 +425,12 @@
         ring_step(rings[2 * piece + 1], step)
 
     wait(gp_in[0], gp0.at[inner])
+    terms(turned(gp0, 0, FP), zt0)
     both_ways(0, 0)
+    terms(jnp.concatenate([turned(gp0, FP, FP + FL)] * per, axis=0), zt3)
     both_ways(3, 0)
     wait(gp_in[1], gp1.at[inner])
+    terms(turned(gp1, 0, FP), zt1)
     both_ways(1, 0)
     wait(pg_in, pr_g)
     sg_out, sg_in = outgoing(sb_g), new()
@@ -427,8 +442,18 @@
     both_ways(0, 1)
     both_ways(3, 1)
     wait(gp_in[2], gp2.at[inner])
+    terms(turned(gp2, 0, FP), zt2)
     both_ways(2, 0)
     both_ways(1, 1)
+    both_ways(0, 2)
+    both_ways(3, 2)
+    both_ways(2, 1)
+    both_ways(1, 2)
+    both_ways(0, 3)
+    both_ways(3, 3)
+    both_ways(2, 2)
+    both_ways(1, 3)
+    both_ways(2, 3)
 
     main = out_sum(3)
     wait(so_in, rb_o)
@@ -440,11 +465,6 @@
     emb_v[...] = jnp.where(filled, placed_v[...] + scale_here * branch, 0.0).astype(BF)
     store_emb = pltpu.make_async_copy(emb_v, emb_out, osem.at[0])
     store_emb.start()
-
-    both_ways(0, 2)
-    both_ways(3, 2)
-    both_ways(2, 1)
-    both_ways(1, 2)
 
     main, tail = grad_sum(3)
     wait(sg_in, rb_g)
@@ -460,11 +480,6 @@
     store_tg = pltpu.make_async_copy(tg_v, tg_out, osem.at[1])
     store_tg.start()
 
-    both_ways(0, 3)
-    both_ways(3, 3)
-    both_ways(2, 2)
-    both_ways(1, 3)
-
     def ring_end(piece):
         value = rings[2 * piece][0][0](0)
         for (_, _, rbuf, _, length, base), _, got in rings[2 * piece : 2 * piece + 2]:
@@ -473,7 +488,6 @@
         return value
 
     wg_v[:, :FP] = ring_end(0)[:CH].astype(BF)
-    both_ways(2, 3)
     folded = ring_end(3)
     unfolded = [folded[:, g * FL : (g + 1) * FL] for g in range(per)]
     rest = jnp.concatenate(unfolded, axis=0)[:CH]
@@ -525,7 +539,7 @@
     NZ, W, F, T, DP = (s[k] for k in ("NZ", "W", "F", "T", "DP"))
     FP, FL, CB, CH, CP, XW, LW = (s[k] for k in ("FP", "FL", "CB", "CH", "CP", "XW", "LW"))
     D = W * 2 * RING
-    n_copies = 66
+    n_copies = 68
     folded = (round_up(-(-CP // (128 // FL)), 16), 128)
     hbm = pl.BlockSpec(memory_space=pl.ANY)
     scratch = [
@@ -553,10 +567,11 @@
         pltpu.VMEM((F, T), BF),
         pltpu.VMEM((F, T), BF),
         pltpu.VMEM((F, T), F32),
+        pltpu.VMEM((F, T), F32),
         pltpu.VMEM((D, T), F32),
         pltpu.VMEM((D, T), F32),
         pltpu.VMEM((CB * CP, W), BF),
-        pltpu.VMEM((RING - 1, CP, T), BF),
+        pltpu.VMEM((RING, CP, T), BF),
         pltpu.VMEM((RING, 2 * CB, CP, T), BF),
         pltpu.VMEM((RING, FP + FL, T), BF),
         pltpu.VMEM((RING, FP, T), BF),
@@ -570,6 +585,9 @@
         pltpu.VMEM((3, XW, T), BF),
         pltpu.VMEM((3, XW, T), BF),
     ]
+    scratch.append(pltpu.VMEM((NZ * CP, RING * T), BF))
+    scratch += [pltpu.VMEM((NZ, CP, FP), F32) for _ in range(3)]
+    scratch.append(pltpu.VMEM((NZ, CP, 128), F32))
     for _ in range(6):
         scratch.append(pltpu.VMEM((NZ, CP, FP), BF))
     for _ in range(2):

time: 63 us -> 60.4 us (0.959)
  Pallas kernels: 62.3 us -> 59.5 us
    pallas_call x1, Pallas kernels: 60.5 us -> 57.7 us  [local(): pl.pallas_call(functools.partial(kernel, s, n_copies), out_shape=(jax.Sha...]
where the time goes in v5:
time: 60.4 us; the launch traced here: 60.1 us
  Pallas kernels  59.5 us (99%)
  between operations  0.64 us (1%)
    pallas_call x1, Pallas kernels, local(): pl.pallas_call(functools.partial(kernel, s, n_copies), out_shape=(jax.Sha...  57.7 us
    pallas_call x1, Pallas kernels, hand_over(): pl.pallas_call(hand_over_kernel, out_shape=tuple((jax.ShapeDtypeStruct(a....  1.78 us

profile of v5, /device:TPU:32, one launch (start us, length us, event | category | flops | bytes accessed | tf_op | source)
XLA Modules:
  0.0 60.1 jit_solution(13033207064824532323)
XLA Ops:
  0.6 57.7 %shard_map.103 = (bf16[128,400]{1,0:T(8,128)(2,1)}, bf16[128,400]{1,0:T(8,128)(2,1)}, bf16[100,800]{1,0:T(8,128)(2,1)}) custom-call(s32[512]{0:T(512)} %enc_hbm.1, s32[64]{0:T(128)} %cnt_hbm.1, bf16[128,400]{1,0:T(8,128)(2,1)} %bitcast.8, bf16[128,400]{1,0:T(8,128)(2,1)} %bitcast.9, f32[3200]{0:T(1024)} %gain_hbm.1, f32[3200]{0:T(1024)} %scale_hbm.1, ...), custom_call_target="tpu_custom_call" | custom-call | tf_op jit(solution)/shard_map/pallas_call | solution.py:600
  58.4 1.8 %shard_map.104 = (bf16[128,400]{1,0:T(8,128)(2,1)}, bf16[128,400]{1,0:T(8,128)(2,1)}, bf16[100,800]{1,0:T(8,128)(2,1)}) custom-call(bf16[128,400]{1,0:T(8,128)(2,1)} %get-tuple-element.9.a, bf16[128,400]{1,0:T(8,128)(2,1)} %get-tuple-element.10.b, bf16[100,800]{1,0:T(8,128)(2,1)} %get-tuple-element.11.c), custom_call_target="tpu_custom_call" | custom-call | tf_op jit(solution)/shard_map/pallas_call | solution.py:523

commit v6 on v5

--- a/solution.py
+++ b/solution.py
@@ -275,15 +275,17 @@
 
         @pl.when(c == parity)
         def _():
+            starts = [(2 * at + parity) * W for at in range(RING)]
+            rows = jnp.concatenate([x_all[lo : lo + W] for lo in starts], axis=1)
+            moved = jnp.dot(sel_y, rows, preferred_element_type=F32).astype(BF)
             for at in range(RING):
-                lo = (2 * at + parity) * W
-                moved = jnp.dot(sel_y, x_all[lo : lo + W], preferred_element_type=F32)
-                px[at] = moved.astype(BF)
+                px[at] = moved[:, at * T : (at + 1) * T]
 
     part_y = c * CB + y
-    xq_out, xq_in = outgoing(px.at[pl.ds(0, RING - 1)]), new()
+    xq_out = outgoing(px.at[pl.ds(0, RING - 1)])
+    xq_in = {way: new() for way in ways}
     for way in ways:
-        send(px.at[(x + way) % RING], xq.at[way, part_y], at_x(way), xq_out, xq_in)
+        send(px.at[(x + way) % RING], xq.at[way, part_y], at_x(way), xq_out, xq_in[way])
     load_up.wait()
     wait(x_pair, x_all.at[four])
     wait(sq_in, sq_ring.at[inner])
@@ -313,16 +315,18 @@
         gp_in.append(got)
         dots = dots + dot
     dots = jnp.broadcast_to(dots / D, (16, T))
-    wait(xq_in, px.at[pl.ds(0, RING - 1)])
+    xq[0, mine] = quarter(x * 2 + c)
+    xq[0, theirs] = quarter(x * 2 + other)
     share_out, share_in = outgoing(xq.at[inner, mine]), new()
+    xq_y_out = outgoing(xq.at[inner, inner])
+    xq_y_in = {k: new() for k in ways}
+    for way in (1, 3, 2):
+        piece = xq.at[way, part_y]
+        wait(xq_in[way], piece)
+        for k in ways:
+            send(piece, piece, at_y(k), xq_y_out, xq_y_in[k])
     piece = xq.at[inner, part_y]
     send(piece, piece, partner, share_out, share_in)
-    xq_y_out = outgoing(xq.at[inner, inner])
-    xq_y_in = {k: new() for k in ways}
-    for k in ways:
-        send(piece, piece, at_y(k), xq_y_out, xq_y_in[k])
-    xq[0, mine] = quarter(x * 2 + c)
-    xq[0, theirs] = quarter(x * 2 + other)
 
     out_t[...] = first_dims(down_v[...], hid_v[...])
 
@@ -539,7 +543,7 @@
     NZ, W, F, T, DP = (s[k] for k in ("NZ", "W", "F", "T", "DP"))
     FP, FL, CB, CH, CP, XW, LW = (s[k] for k in ("FP", "FL", "CB", "CH", "CP", "XW", "LW"))
     D = W * 2 * RING
-    n_copies = 68
+    n_copies = 70
     folded = (round_up(-(-CP // (128 // FL)), 16), 128)
     hbm = pl.BlockSpec(memory_space=pl.ANY)
     scratch = [

time: 60.4 us -> 60.4 us (level)
  no operation moved by 1% of the time
where the time goes in v6:
time: 60.4 us; the launch traced here: 60.3 us
  Pallas kernels  59.7 us (99%)
  between operations  0.64 us (1%)
    pallas_call x1, Pallas kernels, local(): pl.pallas_call(functools.partial(kernel, s, n_copies), out_shape=(jax.Sha...  57.9 us
    pallas_call x1, Pallas kernels, hand_over(): pl.pallas_call(hand_over_kernel, out_shape=tuple((jax.ShapeDtypeStruct(a....  1.78 us

profile of v6, /device:TPU:32, one launch (start us, length us, event | category | flops | bytes accessed | tf_op | source)
XLA Modules:
  0.0 60.3 jit_solution(2002338531295889516)
XLA Ops:
  0.6 57.9 %shard_map.103 = (bf16[128,400]{1,0:T(8,128)(2,1)}, bf16[128,400]{1,0:T(8,128)(2,1)}, bf16[100,800]{1,0:T(8,128)(2,1)}) custom-call(s32[512]{0:T(512)} %enc_hbm.1, s32[64]{0:T(128)} %cnt_hbm.1, bf16[128,400]{1,0:T(8,128)(2,1)} %bitcast.8, bf16[128,400]{1,0:T(8,128)(2,1)} %bitcast.9, f32[3200]{0:T(1024)} %gain_hbm.1, f32[3200]{0:T(1024)} %scale_hbm.1, ...), custom_call_target="tpu_custom_call" | custom-call | tf_op jit(solution)/shard_map/pallas_call | solution.py:604
  58.5 1.8 %shard_map.104 = (bf16[128,400]{1,0:T(8,128)(2,1)}, bf16[128,400]{1,0:T(8,128)(2,1)}, bf16[100,800]{1,0:T(8,128)(2,1)}) custom-call(bf16[128,400]{1,0:T(8,128)(2,1)} %get-tuple-element.9.a, bf16[128,400]{1,0:T(8,128)(2,1)} %get-tuple-element.10.b, bf16[100,800]{1,0:T(8,128)(2,1)} %get-tuple-element.11.c), custom_call_target="tpu_custom_call" | custom-call | tf_op jit(solution)/shard_map/pallas_call | solution.py:527
